TPU v7x, 32 devices: a whole 2x2x4 slice. The times are simulated.
32 devices in a mesh: grp: 2 (over y), ctx: 4 (over z), head: 4 (over x, core).
Axes of the slice: x: 2, y: 2, z: 4, core: 2. Of those that a mesh axis runs over, the one named last changes fastest.
Arguments:
- queries: bfloat16 [16384, 2048], P(('grp', 'ctx', 'head')), parts along dimension 0, may hold values from -6 to 6
- keys: bfloat16 [16384, 2048], P(('grp', 'ctx', 'head')), parts along dimension 0, may hold values from -6 to 6
- values: bfloat16 [16384, 2048], P(('grp', 'ctx', 'head')), parts along dimension 0, may hold values from -6 to 6
- out_grad: bfloat16 [16384, 2048], P(('grp', 'ctx', 'head')), parts along dimension 0, may hold values from -6 to 6
- level_table: float32 [8, 21, 16], P(None, None, 'head'), may hold values from 0.25 to 2
- selector: int32 [256], P(('grp', 'ctx')), parts along dimension 0, may hold values from 0 to 7
Outputs:
- attn_out: bfloat16 [16384, 2048], P(('grp', 'ctx', 'head')), parts along dimension 0
- query_grad: bfloat16 [16384, 2048], P(('grp', 'ctx', 'head')), parts along dimension 0
- key_grad: bfloat16 [16384, 2048], P(('grp', 'ctx', 'head')), parts along dimension 0
- value_grad: bfloat16 [16384, 2048], P(('grp', 'ctx', 'head')), parts along dimension 0
There are 2 independent parts, one for each index of `grp`. A program takes and returns all parts, laid end to end along the dimension named above; an argument that names none is the same for every part. Nothing has to cross between parts.
Inputs may be any that keep to these rules, and one draw needn't show every extreme that they name: `selector`: each stretch's row of the weight table.
All inputs are finite; a program needn't handle non-finite values.
Results may differ from a plain program's by a relative error of at most 0.0051.
Values may be sent and summed in bfloat16 or wider, within the bound.
A program may use at most 256 MiB of HBM per device.

v0:
```python
import math

import jax
import jax.numpy as jnp
from jax import lax
from jax.sharding import PartitionSpec as P

HIGHEST = lax.Precision.HIGHEST


def level_of(xor_value, limit):
    count = jnp.zeros(xor_value.shape, jnp.int32)
    power = 1
    while power < limit:
        count = count + (xor_value >= power).astype(jnp.int32)
        power = power * 2
    return count


def level_weights(level_table, selector, head_width):
    table_rows = jnp.arange(level_table.shape[0], dtype=jnp.int32)
    onehot = (selector[:, None] == table_rows[None, :]).astype(jnp.float32)
    per_stretch = jnp.einsum("cs,slh->clh", onehot, level_table, precision=HIGHEST)
    level_ids = jnp.arange(level_table.shape[1], dtype=jnp.int32).astype(jnp.float32)
    scaling = jnp.exp2(-0.5 * jnp.maximum(level_ids - 1.0, 0.0)) / math.sqrt(head_width)
    return per_stretch * scaling[None, :, None]


def shards(queries, keys, values, out_grad, level_table, selector):
    query_flat, key_flat, value_flat, grad_flat = (
        lax.all_to_all(queries, "head", split_axis=1, concat_axis=0, tiled=True),
        lax.all_to_all(keys, "head", split_axis=1, concat_axis=0, tiled=True),
        lax.all_to_all(values, "head", split_axis=1, concat_axis=0, tiled=True),
        lax.all_to_all(out_grad, "head", split_axis=1, concat_axis=0, tiled=True),
    )
    heads_here = level_table.shape[2]
    tok_count = query_flat.shape[0]
    head_width = query_flat.shape[1] // heads_here
    head_shape = (tok_count, heads_here, head_width)
    query_heads = query_flat.reshape(head_shape)
    key_heads = key_flat.reshape(head_shape)
    value_heads = value_flat.reshape(head_shape)
    grad_heads = grad_flat.reshape(head_shape)
    stretch_count = selector.shape[0]
    stretch_len = tok_count // stretch_count
    per_stretch = level_weights(level_table, selector, head_width)
    lower = tok_count.bit_length() - 1
    token_weights = jnp.repeat(
        jnp.transpose(per_stretch[:, : lower + 1, :], (2, 0, 1)), stretch_len, axis=1
    )
    block_rows = min(512, tok_count)
    positions = jnp.arange(tok_count, dtype=jnp.int32)
    out_parts = []
    query_parts = []
    key_total = jnp.zeros(head_shape, jnp.float32)
    value_total = jnp.zeros(head_shape, jnp.float32)
    for block_index in range(tok_count // block_rows):
        start = block_index * block_rows
        finish = start + block_rows
        query_block = query_heads[start:finish]
        grad_block = grad_heads[start:finish]
        key_part = key_heads[:finish]
        value_part = value_heads[:finish]
        row_pos = positions[start:finish]
        col_pos = positions[:finish]
        level_index = level_of(jnp.bitwise_xor(row_pos[:, None], col_pos[None, :]), tok_count)
        row_weights = token_weights[:, start:finish, :]
        weight = jnp.zeros((heads_here, block_rows, finish), jnp.float32)
        for level_id in range(lower + 1):
            weight = jnp.where(
                (level_index == level_id)[None], row_weights[:, :, level_id][:, :, None], weight
            )
        weight = jnp.where((col_pos[None, :] <= row_pos[:, None])[None], weight, 0.0)
        scores = jnp.einsum(
            "thd,shd->hts", query_block, key_part, preferred_element_type=jnp.float32
        )
        attn_weights = (scores * weight).astype(jnp.bfloat16)
        out_parts.append(
            jnp.einsum("hts,shd->thd", attn_weights, value_part, preferred_element_type=jnp.float32)
        )
        grad_scores = jnp.einsum(
            "thd,shd->hts", grad_block, value_part, preferred_element_type=jnp.float32
        )
        score_grads = (grad_scores * weight).astype(jnp.bfloat16)
        query_parts.append(
            jnp.einsum("hts,shd->thd", score_grads, key_part, preferred_element_type=jnp.float32)
        )
        padding = ((0, tok_count - finish), (0, 0), (0, 0))
        key_total = key_total + jnp.pad(
            jnp.einsum(
                "hts,thd->shd", score_grads, query_block, preferred_element_type=jnp.float32
            ),
            padding,
        )
        value_total = value_total + jnp.pad(
            jnp.einsum(
                "hts,thd->shd", attn_weights, grad_block, preferred_element_type=jnp.float32
            ),
            padding,
        )
    out_local = jnp.concatenate(out_parts, axis=0)
    query_local = jnp.concatenate(query_parts, axis=0)
    stretch_shape = (stretch_count, stretch_len, heads_here, head_width)
    stretch_query = query_heads.reshape(stretch_shape)
    stretch_grad = grad_heads.reshape(stretch_shape)
    block_state = jnp.einsum(
        "shd,she->hde", key_heads, value_heads, preferred_element_type=jnp.float32
    )
    stretch_outer = jnp.einsum(
        "cthd,cthe->chde", stretch_query, stretch_grad, preferred_element_type=jnp.float32
    )
    bits = lax.axis_size("ctx").bit_length() - 1
    cross_weights = per_stretch[:, lower + 1 : lower + 1 + bits, :]
    adjoint_terms = jnp.einsum("cjh,chde->jhde", cross_weights, stretch_outer, precision=HIGHEST)
    position = lax.axis_index("ctx")
    packet = jnp.concatenate([block_state[None], adjoint_terms], axis=0)
    gathered = lax.all_gather(packet, "ctx", axis=0, tiled=True)
    ranks = lax.axis_size("ctx")
    gathered = gathered.reshape(ranks, bits + 1, heads_here, head_width, head_width)
    bit_ids = jnp.arange(bits, dtype=jnp.int32)
    rank_ids = jnp.arange(ranks, dtype=jnp.int32)
    upper_bits = position >> bit_ids & 1
    low_start = position >> bit_ids + 1 << bit_ids + 1
    span_size = jnp.left_shift(jnp.ones_like(bit_ids), bit_ids)
    inside_low = (rank_ids[None, :] >= low_start[:, None]) & (
        rank_ids[None, :] < (low_start + span_size)[:, None]
    )
    inside_high = (rank_ids[None, :] >= (low_start + span_size)[:, None]) & (
        rank_ids[None, :] < (low_start + 2 * span_size)[:, None]
    )
    forward_mask = (inside_low & (upper_bits[:, None] == 1)).astype(jnp.float32)
    backward_mask = (inside_high & (upper_bits[:, None] == 0)).astype(jnp.float32)
    level_stack = jnp.einsum("jn,nhde->jhde", forward_mask, gathered[:, 0], precision=HIGHEST)
    returned = jnp.einsum("jn,njhde->hde", backward_mask, gathered[:, 1:], precision=HIGHEST)
    mixed = jnp.einsum("cjh,jhde->chde", cross_weights, level_stack, precision=HIGHEST).astype(
        jnp.bfloat16
    )
    returned_low = returned.astype(jnp.bfloat16)
    out_cross = jnp.einsum(
        "cthd,chde->cthe", stretch_query, mixed, preferred_element_type=jnp.float32
    ).reshape(head_shape)
    query_cross = jnp.einsum(
        "cthe,chde->cthd", stretch_grad, mixed, preferred_element_type=jnp.float32
    ).reshape(head_shape)
    key_cross = jnp.einsum(
        "she,hde->shd", value_heads, returned_low, preferred_element_type=jnp.float32
    )
    value_cross = jnp.einsum(
        "shd,hde->she", key_heads, returned_low, preferred_element_type=jnp.float32
    )
    flat_shape = (tok_count, heads_here * head_width)
    attn_rows = (out_local + out_cross).astype(jnp.bfloat16).reshape(flat_shape)
    query_rows = (query_local + query_cross).astype(jnp.bfloat16).reshape(flat_shape)
    key_rows = (key_total + key_cross).astype(jnp.bfloat16).reshape(flat_shape)
    value_rows = (value_total + value_cross).astype(jnp.bfloat16).reshape(flat_shape)
    return (
        lax.all_to_all(attn_rows, "head", split_axis=0, concat_axis=1, tiled=True),
        lax.all_to_all(query_rows, "head", split_axis=0, concat_axis=1, tiled=True),
        lax.all_to_all(key_rows, "head", split_axis=0, concat_axis=1, tiled=True),
        lax.all_to_all(value_rows, "head", split_axis=0, concat_axis=1, tiled=True),
    )


def solution(mesh):
    in_specs = (
        P(("grp", "ctx", "head"), None),
        P(("grp", "ctx", "head"), None),
        P(("grp", "ctx", "head"), None),
        P(("grp", "ctx", "head"), None),
        P(None, None, "head"),
        P(("grp", "ctx")),
    )
    out_specs = (
        P(("grp", "ctx", "head"), None),
        P(("grp", "ctx", "head"), None),
        P(("grp", "ctx", "head"), None),
        P(("grp", "ctx", "head"), None),
    )
    return jax.shard_map(shards, mesh=mesh, in_specs=in_specs, out_specs=out_specs, check_vma=False)
```

profile of v0, /device:TPU:0, one launch (start us, length us, event | category | flops | bytes accessed | tf_op | source)
XLA Modules:
  0.0 549.9 jit_solution(6099098687646648184)
XLA Ops:
  11.1 4.2 all-to-all-start
  19.3 10.5 %broadcast_compare_fusion.24 = (pred[512,1536]{1,0:T(8,128)(4,1)}, pred[512,1536]{1,0:T(8,128)(4,1)}, pred[512,1536]{1,0:T(8,128)(4,1)}, pred[512,1536]{1,0:T(8,...) fusion(s32[1536]{0:T(1024)S(1)} %iota_add_fusion, ...), kind=kLoop, calls=%fused_computation.118 | loop fusion | flops 36175872 | bytes 10231808 | tf_op jit(solution)/shard_map/le | solution.py:73
  29.8 11.2 %all-to-all-done = bf16[512,4,512]{0,2,1:T(8,128)(2,1)S(1)} async-done(((bf16[512,4,512]{0,2,1:T(8,128)(2,1)}), bf16[512,4,512]{0,2,1:T(8,128)(2,1)S(1)}, u32[]{:S(2)}, u32[]{:S(2)}) %all-to-all-start) | async-done | bytes 2097184 | tf_op jit(solution)/shard_map/all_to_all | solution.py:31
  46.0 15.1 %iota_compare_fusion = (pred[512,2048]{1,0:T(8,128)(4,1)}, pred[512,2048]{1,0:T(8,128)(4,1)}, pred[512,2048]{1,0:T(8,128)(4,1)}, pred[512,2048]{1,0:T(8,128)(4,1...) fusion(s32[512]{0:T(512)S(1)} %iota_add_fusion.2), kind=kLoop, calls=%fused_computation.69 | loop fusion | flops 48234496 | bytes 13633536 | tf_op jit(solution)/shard_map/le | solution.py:73
  71.6 4.5 all-to-all-start.2
  78.1 4.2 broadcast_compare_fusion.50
  82.3 19.5 %all-to-all-done.2 = bf16[512,4,512]{2,0,1:T(8,128)(2,1)} async-done(((bf16[512,4,512]{2,0,1:T(8,128)(2,1)}), bf16[512,4,512]{2,0,1:T(8,128)(2,1)}, u32[]{:S(2)}, u32[]{:S(2)}) %all-to-all-start.2) | async-done | bytes 2097184 | tf_op jit(solution)/shard_map/all_to_all | solution.py:33
  101.8 4.5 all-to-all-start.3
  106.8 8.4 %broadcast_compare_fusion.37 = (pred[512,1024]{1,0:T(8,128)(4,1)}, pred[512,1024]{1,0:T(8,128)(4,1)}, pred[512,1024]{1,0:T(8,128)(4,1)}, pred[512,1024]{1,0:T(8,...) fusion(s32[1024]{0:T(1024)S(1)} %iota_add_fusion.1, ...), kind=kLoop, calls=%fused_computation.141 | loop fusion | flops 24117248 | bytes 6821888 | tf_op jit(solution)/shard_map/le | solution.py:73
  134.3 4.3 copy.218
  149.9 4.8 copy.324
  154.8 5.4 reshape.1384
  172.4 4.3 reshape_reshape.7
  177.0 8.1 %multiply_convert_fusion.6 = bf16[4,512,512]{2,1,0:T(8,128)(2,1)S(1)} fusion(bf16[512,4,128]{0,2,1:T(8,128)(2,1)} %bitcast.305, bf16[512,4,128]{0,2,1:T(8,128)(2,1)} %bitcast.298, f32[4,512]{1,0:T(4,128)S(1)} %copy-done.116, f32[4,512]{1,0:T(4,128)} %get-tuple-element.60, f32[4,512]{1,0:T(4,128)} %get-tuple-element.61, f32[4,512]{1,0:T(4,128)} %get-tuple-element.62, ...), kind=kOutput, calls=%fused_computation.53 | convolution fusion | flops 284164096 | bytes 6651904 | tf_op jit(solution)/shard_map/thd,shd->hts/dot_general | solution.py:81
  185.5 6.6 %multiply_convert_fusion.7 = bf16[4,512,512]{2,1,0:T(8,128)(2,1)S(1)} fusion(bf16[512,4,128]{0,2,1:T(8,128)(2,1)S(1)} %bitcast.310, bf16[512,4,128]{0,2,1:T(8,128)(2,1)S(1)} %bitcast.296, f32[4,512]{1,0:T(4,128)S(1)} %copy-done.116, f32[4,512]{1,0:T(4,128)S(1)} %copy-done.117, f32[4,512]{1,0:T(4,128)S(1)} %copy-done.118, f32[4,512]{1,0:T(4,128)S(1)} %copy-done.119, ...), kind=kOutput, calls=%fused_computation.70 | convolution fusion | flops 284164096 | bytes 6651904 | tf_op jit(solution)/shard_map/thd,shd->hts/dot_general | solution.py:74
  196.7 12.1 %multiply_convert_fusion.4 = bf16[4,512,1024]{2,1,0:T(8,128)(2,1)S(1)} fusion(f32[4,512]{1,0:T(4,128)S(1)} %copy-done.103, f32[4,512]{1,0:T(4,128)S(1)} %copy-done.104, f32[4,512]{1,0:T(4,128)S(1)} %copy-done.105, f32[4,512]{1,0:T(4,128)S(1)} %copy-done.106, f32[4,512]{1,0:T(4,128)S(1)} %copy-done.107, f32[4,512]{1,0:T(4,128)S(1)} %copy-done.108, ...), kind=kOutput, calls=%fused_computation.30 | convolution fusion | flops 568328192 | bytes 12681216 | tf_op jit(solution)/shard_map/thd,shd->hts/dot_general | solution.py:81
  208.9 11.5 %multiply_convert_fusion.5 = bf16[4,512,1024]{2,1,0:T(8,128)(2,1)S(1)} fusion(f32[4,512]{1,0:T(4,128)S(1)} %copy-done.103, f32[4,512]{1,0:T(4,128)S(1)} %copy-done.104, f32[4,512]{1,0:T(4,128)S(1)} %copy-done.105, f32[4,512]{1,0:T(4,128)S(1)} %copy-done.106, f32[4,512]{1,0:T(4,128)S(1)} %copy-done.107, f32[4,512]{1,0:T(4,128)S(1)} %copy-done.108, ...), kind=kOutput, calls=%fused_computation.31 | convolution fusion | flops 568328192 | bytes 12681216 | tf_op jit(solution)/shard_map/thd,shd->hts/dot_general | solution.py:74
  226.9 9.5 %fusion.37 = f32[2,4,128,128]{3,0,2,1:T(2,128)S(1)} fusion(f32[32,4,128,128]{3,2,1,0:T(8,128)S(1)} %fusion.28, f32[32,21,4]{0,1,2:T(8,128)S(1)} %convolution_multiply_fusion), kind=kOutput, calls=%fused_computation.124 | convolution fusion | flops 50331648 | bytes 8916992 | tf_op jit(solution)/shard_map/cjh,chde->jhde/dot_general | solution.py:114
  239.0 19.7 %multiply_convert_fusion.2 = bf16[4,512,1536]{2,1,0:T(8,128)(2,1)S(1)} fusion(bf16[512,4,128]{0,2,1:T(8,128)(2,1)S(1)} %bitcast.304, f32[4,512]{1,0:T(4,128)S(1)} %get-tuple-element.33, f32[4,512]{1,0:T(4,128)S(1)} %get-tuple-element.34, f32[4,512]{1,0:T(4,128)S(1)} %get-tuple-element.35, f32[4,512]{1,0:T(4,128)S(1)} %get-tuple-element.36, ...), kind=kOutput, calls=%fused_computation.14 | convolution fusion | flops 852492288 | bytes 18710528 | tf_op jit(solution)/shard_map/thd,shd->hts/dot_general | solution.py:81
  258.9 18.2 %multiply_convert_fusion.3 = bf16[4,512,1536]{2,1,0:T(8,128)(2,1)S(1)} fusion(bf16[512,4,128]{0,2,1:T(8,128)(2,1)S(1)} %bitcast.311, bf16[1536,4,128]{0,2,1:T(8,128)(2,1)S(1)} %copy-done.44, f32[4,512]{1,0:T(4,128)S(1)} %get-tuple-element.33, f32[4,512]{1,0:T(4,128)S(1)} %get-tuple-element.34, f32[4,512]{1,0:T(4,128)S(1)} %get-tuple-element.35, ...), kind=kOutput, calls=%fused_computation.15 | convolution fusion | flops 852492288 | bytes 18710528 | tf_op jit(solution)/shard_map/thd,shd->hts/dot_general | solution.py:74
  283.7 26.3 %multiply_convert_fusion.1 = bf16[4,512,2048]{2,1,0:T(8,128)(2,1)S(1)} fusion(f32[4,512]{1,0:T(4,128)S(1)} %copy-done.89, f32[4,512]{1,0:T(4,128)S(1)} %copy-done.90, f32[4,512]{1,0:T(4,128)S(1)} %copy-done.91, f32[4,512]{1,0:T(4,128)S(1)} %copy-done.92, f32[4,512]{1,0:T(4,128)S(1)} %copy-done.93, f32[4,512]{1,0:T(4,128)S(1)} %copy-done.94, ...), kind=kOutput, calls=%fused_computation.12 | convolution fusion | flops 1136656384 | bytes 24739840 | tf_op jit(solution)/shard_map/thd,shd->hts/dot_general | solution.py:74
  316.7 5.4 copy.213
  322.1 25.2 %multiply_convert_fusion = bf16[4,512,2048]{2,1,0:T(8,128)(2,1)S(1)} fusion(f32[4,512]{1,0:T(4,128)S(1)} %copy-done.89, f32[4,512]{1,0:T(4,128)S(1)} %copy-done.90, f32[4,512]{1,0:T(4,128)S(1)} %copy-done.91, f32[4,512]{1,0:T(4,128)S(1)} %copy-done.92, f32[4,512]{1,0:T(4,128)S(1)} %copy-done.93, f32[4,512]{1,0:T(4,128)S(1)} %copy-done.94, ...), kind=kOutput, calls=%fused_computation.11 | convolution fusion | flops 1136656384 | bytes 24739840 | tf_op jit(solution)/shard_map/thd,shd->hts/dot_general | solution.py:81
  353.8 5.8 %copy.240 = f32[2048,512]{1,0:T(8,128)} copy(f32[2048,512]{0,1:T(8,128)} %pad_maximum_fusion.1) | data formatting | bytes 8388608 | tf_op jit(solution)/shard_map/concatenate | solution.py:102
  359.6 5.1 convolution_bitcast_fusion.3
  364.7 6.8 %convolution_bitcast_fusion.1 = f32[1536,4,128]{2,0,1:T(8,128)} fusion(bf16[4,512,1536]{2,1,0:T(8,128)(2,1)} %copy-done.25, bf16[512,4,128]{0,2,1:T(8,128)(2,1)S(1)} %bitcast.312), kind=kOutput, calls=%fused_computation.77 | convolution fusion | flops 805306368 | bytes 9961472 | tf_op jit(solution)/shard_map/hts,thd->shd/dot_general | solution.py:90
  374.6 7.2 %convert_bitcast_fusion = bf16[32,4,128,128]{3,0,2,1:T(8,128)(2,1)S(1)} fusion(f32[2,4,128,128]{3,0,2,1:T(2,128)S(1)} %fusion.40, f32[32,21,4]{0,1,2:T(8,128)S(1)} %copy-done.88), kind=kOutput, calls=%fused_computation.55 | convolution fusion | flops 52428800 | bytes 4722688 | tf_op jit(solution)/shard_map/cjh,jhde->chde/dot_general | solution.py:135
  381.8 4.6 fusion.22
  386.4 5.5 %copy.243 = f32[32,64,4,128]{3,2,1,0:T(4,128)} copy(f32[32,64,4,128]{3,1,2,0:T(8,128)S(1)} %fusion.22) | data formatting | bytes 8388608 | tf_op jit(solution)/shard_map/cthe,chde->cthd/transpose | solution.py:142
  391.9 5.5 reshape.1375
  397.4 5.5 %add_convert_fusion = bf16[4,512,512]{2,1,0:T(8,128)(2,1)} fusion(f32[4,512,512]{2,1,0:T(8,128)} %bitcast.280, f32[4,512,512]{2,1,0:T(8,128)} %reshape.1375), kind=kLoop, calls=%fused_computation.52 | loop fusion | flops 2097152 | bytes 10485760 | tf_op jit(solution)/shard_map/convert_element_type | solution.py:153
  402.9 4.7 all-to-all-start.5
  410.2 8.6 %fusion.69 = f32[4,2048,128]{2,1,0:T(8,128)} fusion(bf16[4,512,2048]{2,1,0:T(8,128)(2,1)} %copy-done.20, bf16[512,4,128]{0,2,1:T(8,128)(2,1)} %bitcast.307), kind=kOutput, calls=%fused_computation.247 | convolution fusion | flops 1073741824 | bytes 13107200 | tf_op jit(solution)/shard_map/hts,thd->shd/dot_general | solution.py:90
  422.9 5.4 fusion.3
  428.3 10.7 %copy.256 = bf16[2048,4,128]{2,1,0:T(4,128)(2,1)} copy(bf16[2048,4,128]{2,0,1:T(8,128)(2,1)S(1)} %fusion.3) | data formatting | bytes 4194304 | tf_op jit(solution)/shard_map/convert_element_type | solution.py:154
  443.1 4.9 all-to-all-start.6
  450.7 5.4 convolution_bitcast_fusion.2
  456.0 4.3 fusion.19
  460.3 5.6 %copy.227 = f32[32,64,4,128]{3,2,1,0:T(4,128)} copy(f32[32,64,4,128]{3,1,2,0:T(8,128)S(1)} %fusion.19) | data formatting | bytes 8388608 | tf_op jit(solution)/shard_map/cthd,chde->cthe/transpose | solution.py:139
  465.9 5.5 reshape.1374
  471.4 5.5 %add_convert_fusion.1 = bf16[4,512,512]{2,1,0:T(8,128)(2,1)} fusion(f32[4,512,512]{2,1,0:T(8,128)} %bitcast.279, f32[4,512,512]{2,1,0:T(8,128)} %reshape.1374), kind=kLoop, calls=%fused_computation.54 | loop fusion | flops 2097152 | bytes 10485760 | tf_op jit(solution)/shard_map/convert_element_type | solution.py:152
  476.9 4.7 all-to-all-start.4
  481.6 5.2 convolution_bitcast_fusion
  486.9 6.6 %fusion.70 = f32[4,2048,128]{2,1,0:T(8,128)S(1)} fusion(bf16[4,512,2048]{2,1,0:T(8,128)(2,1)} %copy-done.19, bf16[512,4,128]{0,2,1:T(8,128)(2,1)S(1)} %bitcast.302), kind=kOutput, calls=%fused_computation.248 | convolution fusion | flops 1073741824 | bytes 13107200 | tf_op jit(solution)/shard_map/hts,thd->shd/dot_general | solution.py:96
  494.9 9.8 %copy.268 = bf16[2048,4,128]{2,1,0:T(4,128)(2,1)S(1)} copy(bf16[2048,4,128]{2,0,1:T(8,128)(2,1)S(1)} %fusion.2) | data formatting | bytes 4194304 | tf_op jit(solution)/shard_map/convert_element_type | solution.py:155
  510.9 4.1 copy.244
  519.0 4.1 copy.257
  527.0 4.1 copy.228
  (350 shorter events, 144.7 us)
Async XLA Ops:
  7.2 53.9 %copy-start = (f32[8,21,4]{1,2,0:T(4,128)S(1)}, f32[8,21,4]{1,2,0:T(4,128)}, u32[]{:S(2)}) copy-start(f32[8,21,4]{1,2,0:T(4,128)} %param.10) | copy-start | bytes 8068
  11.1 29.9 %all-to-all-start = ((bf16[512,4,512]{0,2,1:T(8,128)(2,1)}), bf16[512,4,512]{0,2,1:T(8,128)(2,1)S(1)}, u32[]{:S(2)}, u32[]{:S(2)}) async-start(bf16[512,4,512]{0,2,1:T(8,128)(2,1)} %bitcast.284), calls=%async_computation | async-start | bytes 4194304 | tf_op jit(solution)/shard_map/all_to_all | solution.py:31
  42.3 29.3 %all-to-all-start.1 = ((bf16[512,4,512]{0,2,1:T(8,128)(2,1)}), bf16[512,4,512]{0,2,1:T(8,128)(2,1)S(1)}, u32[]{:S(2)}, u32[]{:S(2)}) async-start(bf16[512,4,512]{0,2,1:T(8,128)(2,1)} %bitcast.283), calls=%async_computation.1 | async-start | bytes 4194304 | tf_op jit(solution)/shard_map/all_to_all | solution.py:32
  46.0 15.1 %copy-start.132 = (s32[32]{0:T(128)S(1)}, s32[32]{0:T(128)}, u32[]{:S(2)}) copy-start(s32[32]{0:T(128)} %param.11) | copy-start | bytes 388
  61.3 165.5 %copy-start.87 = (f32[32,21,4]{0,1,2:T(8,128)}, f32[32,21,4]{0,1,2:T(8,128)S(1)}, u32[]{:S(2)}) copy-start(f32[32,21,4]{0,1,2:T(8,128)S(1)} %convolution_multiply_fusion) | copy-start | bytes 32260
  71.6 30.2 %all-to-all-start.2 = ((bf16[512,4,512]{2,0,1:T(8,128)(2,1)}), bf16[512,4,512]{2,0,1:T(8,128)(2,1)}, u32[]{:S(2)}, u32[]{:S(2)}) async-start(bf16[512,4,512]{2,0,1:T(8,128)(2,1)} %bitcast.282), calls=%async_computation.2 | async-start | bytes 4194304 | tf_op jit(solution)/shard_map/all_to_all | solution.py:33
  101.8 32.5 %all-to-all-start.3 = ((bf16[512,4,512]{0,2,1:T(8,128)(2,1)}), bf16[512,4,512]{0,2,1:T(8,128)(2,1)}, u32[]{:S(2)}, u32[]{:S(2)}) async-start(bf16[512,4,512]{0,2,1:T(8,128)(2,1)} %bitcast.281), calls=%async_computation.3 | async-start | bytes 4194304 | tf_op jit(solution)/shard_map/all_to_all | solution.py:34
  106.3 265.2 %all-gather.2.cloned.1.call-start = ((), (), s32[]{:S(2)}) async-start(), calls=%async_computation.8 | async-start | bytes 3932160 | tf_op jit(solution)/shard_map/all_gather | solution.py:117
  149.9 12.9 %copy-start.4 = (bf16[2048,4,128]{2,1,0:T(4,128)(2,1)}, bf16[2048,4,128]{2,1,0:T(4,128)(2,1)S(1)}, u32[]{:S(2)}) copy-start(bf16[2048,4,128]{2,1,0:T(4,128)(2,1)S(1)} %reshape.1371) | copy-start | bytes 6291460
  172.4 63.9 %copy-start.6 = (bf16[2048,4,128]{0,2,1:T(8,128)(2,1)}, bf16[2048,4,128]{0,2,1:T(8,128)(2,1)S(1)}, u32[]{:S(2)}) copy-start(bf16[2048,4,128]{0,2,1:T(8,128)(2,1)S(1)} %copy.313) | copy-start | bytes 6291460
  176.8 8.4 %copy-start.39 = (bf16[1,512,512]{1,2,0:T(8,128)(2,1)S(1)}, bf16[1,512,512]{1,2,0:T(8,128)(2,1)}, u32[]{:S(2)}) copy-start(bf16[1,512,512]{1,2,0:T(8,128)(2,1)} %get-tuple-element.16) | copy-start | bytes 1572868
  176.8 8.4 %copy-start.75 = (pred[512,512]{1,0:T(8,128)(4,1)S(1)}, pred[512,512]{1,0:T(8,128)(4,1)}, u32[]{:S(2)}) copy-start(pred[512,512]{1,0:T(8,128)(4,1)} %get-tuple-element.95) | copy-start | bytes 786436
  176.8 8.4 %copy-start.76 = (pred[512,512]{1,0:T(8,128)(4,1)S(1)}, pred[512,512]{1,0:T(8,128)(4,1)}, u32[]{:S(2)}) copy-start(pred[512,512]{1,0:T(8,128)(4,1)} %get-tuple-element.96) | copy-start | bytes 786436
  185.4 8.6 %copy-start.34 = (bf16[1,512,512]{1,2,0:T(8,128)(2,1)S(1)}, bf16[1,512,512]{1,2,0:T(8,128)(2,1)}, u32[]{:S(2)}) copy-start(bf16[1,512,512]{1,2,0:T(8,128)(2,1)} %copy.200) | copy-start | bytes 1572868
  185.4 10.4 %copy-start.109 = (f32[4,512]{1,0:T(4,128)S(1)}, f32[4,512]{1,0:T(4,128)}, u32[]{:S(2)}) copy-start(f32[4,512]{1,0:T(4,128)} %get-tuple-element.52) | copy-start | bytes 24580
  185.4 10.4 %copy-start.110 = (f32[4,512]{1,0:T(4,128)S(1)}, f32[4,512]{1,0:T(4,128)}, u32[]{:S(2)}) copy-start(f32[4,512]{1,0:T(4,128)} %get-tuple-element.53) | copy-start | bytes 24580
  185.5 10.4 %copy-start.111 = (f32[4,512]{1,0:T(4,128)S(1)}, f32[4,512]{1,0:T(4,128)}, u32[]{:S(2)}) copy-start(f32[4,512]{1,0:T(4,128)} %get-tuple-element.54) | copy-start | bytes 24580
  196.7 12.2 %copy-start.27 = (bf16[1024,4,128]{0,2,1:T(8,128)(2,1)S(1)}, bf16[1024,4,128]{0,2,1:T(8,128)(2,1)}, u32[]{:S(2)}) copy-start(bf16[1024,4,128]{0,2,1:T(8,128)(2,1)} %reshape.1383) | copy-start | bytes 3145732
  196.7 12.2 %copy-start.42 = (bf16[1,512,512]{1,2,0:T(8,128)(2,1)S(1)}, bf16[1,512,512]{1,2,0:T(8,128)(2,1)}, u32[]{:S(2)}) copy-start(bf16[1,512,512]{1,2,0:T(8,128)(2,1)} %get-tuple-element.19) | copy-start | bytes 1572868
  196.7 12.2 %copy-start.112 = (f32[4,512]{1,0:T(4,128)S(1)}, f32[4,512]{1,0:T(4,128)}, u32[]{:S(2)}) copy-start(f32[4,512]{1,0:T(4,128)} %get-tuple-element.55) | copy-start | bytes 24580
  196.7 12.2 %copy-start.113 = (f32[4,512]{1,0:T(4,128)S(1)}, f32[4,512]{1,0:T(4,128)}, u32[]{:S(2)}) copy-start(f32[4,512]{1,0:T(4,128)} %get-tuple-element.56) | copy-start | bytes 24580
  196.7 12.2 %copy-start.114 = (f32[4,512]{1,0:T(4,128)S(1)}, f32[4,512]{1,0:T(4,128)}, u32[]{:S(2)}) copy-start(f32[4,512]{1,0:T(4,128)} %get-tuple-element.57) | copy-start | bytes 24580
  208.8 11.6 %copy-start.15 = (bf16[4,512,1024]{2,1,0:T(8,128)(2,1)}, bf16[4,512,1024]{2,1,0:T(8,128)(2,1)S(1)}, u32[]{:S(2)}) copy-start(bf16[4,512,1024]{2,1,0:T(8,128)(2,1)S(1)} %multiply_convert_fusion.4) | copy-start | bytes 12582916
  226.8 9.5 %copy-start.21 = (bf16[2048,4,128]{0,2,1:T(8,128)(2,1)S(1)}, bf16[2048,4,128]{0,2,1:T(8,128)(2,1)}, u32[]{:S(2)}) copy-start(bf16[2048,4,128]{0,2,1:T(8,128)(2,1)} %copy.214) | copy-start | bytes 6291460
  238.9 19.9 %copy-start.40 = (bf16[1,512,512]{1,2,0:T(8,128)(2,1)S(1)}, bf16[1,512,512]{1,2,0:T(8,128)(2,1)}, u32[]{:S(2)}) copy-start(bf16[1,512,512]{1,2,0:T(8,128)(2,1)} %get-tuple-element.18) | copy-start | bytes 1572868
  238.9 19.9 %copy-start.44 = (bf16[1536,4,128]{0,2,1:T(8,128)(2,1)S(1)}, bf16[1536,4,128]{0,2,1:T(8,128)(2,1)}, u32[]{:S(2)}) copy-start(bf16[1536,4,128]{0,2,1:T(8,128)(2,1)} %reshape.1384) | copy-start | bytes 4718596
  238.9 19.9 %copy-start.50 = (pred[512,1536]{1,0:T(8,128)(4,1)S(1)}, pred[512,1536]{1,0:T(8,128)(4,1)}, u32[]{:S(2)}) copy-start(pred[512,1536]{1,0:T(8,128)(4,1)} %get-tuple-element.68) | copy-start | bytes 2359300
  238.9 19.9 %copy-start.51 = (pred[512,1536]{1,0:T(8,128)(4,1)S(1)}, pred[512,1536]{1,0:T(8,128)(4,1)}, u32[]{:S(2)}) copy-start(pred[512,1536]{1,0:T(8,128)(4,1)} %get-tuple-element.69) | copy-start | bytes 2359300
  238.9 19.9 %copy-start.52 = (pred[512,1536]{1,0:T(8,128)(4,1)S(1)}, pred[512,1536]{1,0:T(8,128)(4,1)}, u32[]{:S(2)}) copy-start(pred[512,1536]{1,0:T(8,128)(4,1)} %get-tuple-element.70) | copy-start | bytes 2359300
  238.9 19.9 %copy-start.53 = (pred[512,1536]{1,0:T(8,128)(4,1)S(1)}, pred[512,1536]{1,0:T(8,128)(4,1)}, u32[]{:S(2)}) copy-start(pred[512,1536]{1,0:T(8,128)(4,1)} %get-tuple-element.71) | copy-start | bytes 2359300
  238.9 19.9 %copy-start.54 = (pred[512,1536]{1,0:T(8,128)(4,1)S(1)}, pred[512,1536]{1,0:T(8,128)(4,1)}, u32[]{:S(2)}) copy-start(pred[512,1536]{1,0:T(8,128)(4,1)} %get-tuple-element.72) | copy-start | bytes 2359300
  238.9 19.9 %copy-start.55 = (pred[512,1536]{1,0:T(8,128)(4,1)S(1)}, pred[512,1536]{1,0:T(8,128)(4,1)}, u32[]{:S(2)}) copy-start(pred[512,1536]{1,0:T(8,128)(4,1)} %get-tuple-element.73) | copy-start | bytes 2359300
  239.0 19.9 %copy-start.56 = (pred[512,1536]{1,0:T(8,128)(4,1)S(1)}, pred[512,1536]{1,0:T(8,128)(4,1)}, u32[]{:S(2)}) copy-start(pred[512,1536]{1,0:T(8,128)(4,1)} %get-tuple-element.74) | copy-start | bytes 2359300
  239.0 19.9 %copy-start.57 = (pred[512,1536]{1,0:T(8,128)(4,1)S(1)}, pred[512,1536]{1,0:T(8,128)(4,1)}, u32[]{:S(2)}) copy-start(pred[512,1536]{1,0:T(8,128)(4,1)} %get-tuple-element.75) | copy-start | bytes 2359300
  239.0 19.9 %copy-start.58 = (pred[512,1536]{1,0:T(8,128)(4,1)S(1)}, pred[512,1536]{1,0:T(8,128)(4,1)}, u32[]{:S(2)}) copy-start(pred[512,1536]{1,0:T(8,128)(4,1)} %get-tuple-element.76) | copy-start | bytes 2359300
  239.0 19.9 %copy-start.59 = (pred[512,1536]{1,0:T(8,128)(4,1)S(1)}, pred[512,1536]{1,0:T(8,128)(4,1)}, u32[]{:S(2)}) copy-start(pred[512,1536]{1,0:T(8,128)(4,1)} %get-tuple-element.77) | copy-start | bytes 2359300
  239.0 19.9 %copy-start.60 = (pred[512,1536]{1,0:T(8,128)(4,1)S(1)}, pred[512,1536]{1,0:T(8,128)(4,1)}, u32[]{:S(2)}) copy-start(pred[512,1536]{1,0:T(8,128)(4,1)} %get-tuple-element.78) | copy-start | bytes 2359300
  239.0 19.9 %copy-start.61 = (pred[512,1536]{1,0:T(8,128)(4,1)S(1)}, pred[512,1536]{1,0:T(8,128)(4,1)}, u32[]{:S(2)}) copy-start(pred[512,1536]{1,0:T(8,128)(4,1)} %get-tuple-element.79) | copy-start | bytes 2359300
  258.8 18.3 %copy-start.25 = (bf16[4,512,1536]{2,1,0:T(8,128)(2,1)}, bf16[4,512,1536]{2,1,0:T(8,128)(2,1)S(1)}, u32[]{:S(2)}) copy-start(bf16[4,512,1536]{2,1,0:T(8,128)(2,1)S(1)} %multiply_convert_fusion.2) | copy-start | bytes 18874372
  283.7 26.4 %copy-start.7 = (bf16[2048,4,128]{0,2,1:T(8,128)(2,1)S(1)}, bf16[2048,4,128]{0,2,1:T(8,128)(2,1)}, u32[]{:S(2)}) copy-start(bf16[2048,4,128]{0,2,1:T(8,128)(2,1)} %copy-done.6) | copy-start | bytes 6291460
  322.1 25.3 %copy-start.22 = (bf16[2048,4,128]{0,2,1:T(8,128)(2,1)S(1)}, bf16[2048,4,128]{0,2,1:T(8,128)(2,1)}, u32[]{:S(2)}) copy-start(bf16[2048,4,128]{0,2,1:T(8,128)(2,1)} %copy.214) | copy-start | bytes 6291460
  364.7 9.8 %copy-start.88 = (f32[32,21,4]{0,1,2:T(8,128)S(1)}, f32[32,21,4]{0,1,2:T(8,128)}, u32[]{:S(2)}) copy-start(f32[32,21,4]{0,1,2:T(8,128)} %copy-done.87) | copy-start | bytes 32260
  372.9 8.9 %copy-start.13 = (bf16[32,64,4,128]{3,2,1,0:T(4,128)(2,1)S(1)}, bf16[32,64,4,128]{3,2,1,0:T(4,128)(2,1)}, u32[]{:S(2)}) copy-start(bf16[32,64,4,128]{3,2,1,0:T(4,128)(2,1)} %reshape_reshape.7) | copy-start | bytes 6291460
  402.9 40.2 %all-to-all-start.5 = ((bf16[4,512,512]{2,1,0:T(8,128)(2,1)}), bf16[4,512,512]{2,1,0:T(8,128)(2,1)}, u32[]{:S(2)}, u32[]{:S(2)}) async-start(bf16[4,512,512]{2,1,0:T(8,128)(2,1)} %add_convert_fusion), calls=%async_computation.5 | async-start | bytes 4194304 | tf_op jit(solution)/shard_map/all_to_all | solution.py:158
  410.2 8.6 %copy-start.32 = (f32[12,4,128,128]{3,2,1,0:T(8,128)S(1)}, f32[12,4,128,128]{3,2,1,0:T(8,128)}, u32[]{:S(2)}) copy-start(f32[12,4,128,128]{3,2,1,0:T(8,128)} %all-gather.2.cloned.1.call-done) | copy-start | bytes 9437188
  443.1 33.7 %all-to-all-start.6 = ((bf16[4,512,512]{2,1,0:T(8,128)(2,1)}), bf16[4,512,512]{2,1,0:T(8,128)(2,1)}, u32[]{:S(2)}, u32[]{:S(2)}) async-start(bf16[4,512,512]{2,1,0:T(8,128)(2,1)} %all_to_all.118), calls=%async_computation.6 | async-start | bytes 4194304 | tf_op jit(solution)/shard_map/all_to_all | solution.py:159
  476.9 30.4 %all-to-all-start.4 = ((bf16[4,512,512]{2,1,0:T(8,128)(2,1)}), bf16[4,512,512]{2,1,0:T(8,128)(2,1)}, u32[]{:S(2)}, u32[]{:S(2)}) async-start(bf16[4,512,512]{2,1,0:T(8,128)(2,1)} %add_convert_fusion.1), calls=%async_computation.4 | async-start | bytes 4194304 | tf_op jit(solution)/shard_map/all_to_all | solution.py:157
  507.3 29.3 %all-to-all-start.7 = ((bf16[4,512,512]{2,1,0:T(8,128)(2,1)}), bf16[4,512,512]{2,1,0:T(8,128)(2,1)S(1)}, u32[]{:S(2)}, u32[]{:S(2)}) async-start(bf16[4,512,512]{2,1,0:T(8,128)(2,1)} %all_to_all.122), calls=%async_computation.7 | async-start | bytes 4194304 | tf_op jit(solution)/shard_map/all_to_all | solution.py:160
  (94 other events, 477.5 us)
Sparse Core Ops, SparseCore 0:
  239.0 66.0 all-gather.1
where the time goes:
time: 559 us; the launch traced here: 550 us
  matrix products  231 us (41%)
  local copies, waits for them, and re-layouts  177 us (32%)
  other arithmetic  56.1 us (10%)
  starting transfers between devices  35.2 us (6%)
  waiting for transfers between devices  33.6 us (6%)
  between operations  16.2 us (3%)
    dot_general x4, matrix products, shards(): jnp.einsum('thd,shd->hts', grad_block, value_part, preferred_element_type...  65.2 us
    dot_general x4, matrix products, shards(): jnp.einsum('thd,shd->hts', query_block, key_part, preferred_element_type=...  62.6 us
    le x4, other arithmetic, shards(): col_pos[None, :] <= row_pos[:, None]  38.2 us
    unnamed x273, local copies, waits for them, and re-layouts  32.9 us
    dot_general x4, matrix products, shards(): jnp.einsum('hts,thd->shd', score_grads, query_block, preferred_element_ty...  23.1 us
    dot_general x4, matrix products, shards(): jnp.einsum('hts,thd->shd', attn_weights, grad_block, preferred_element_ty...  19.8 us
    all_to_all x1, waiting for transfers between devices, shards(): lax.all_to_all(values, 'head', split_axis=1, concat_axis=0, tiled=True)  19.5 us
    slice x7, local copies, waits for them, and re-layouts, shards(): key_part = key_heads[:finish]  17.2 us
  transfers between devices with their start and end apart: 9, of which 5 were waited for; matrix products, arithmetic and copies ran while one was open for 56% of the time, Pallas kernels for 0%

commit v1 on v0

v1 whole, which is shorter than its diff:
```python
import functools
import math

import jax
import jax.numpy as jnp
from jax import lax
from jax.experimental import pallas as pl
from jax.experimental.pallas import tpu as pltpu
from jax.sharding import PartitionSpec as P

F32 = jnp.float32
BF16 = jnp.bfloat16
STRETCH = 64
TILE = 128
NT = (((1,), (1,)), ((), ()))
TN = (((0,), (0,)), ((), ()))
NN = (((1,), (0,)), ((), ()))
VMEM_LIMIT = 40 * 1024 * 1024


def mm(a, b, dims):
    return lax.dot_general(a, b, dims, preferred_element_type=F32)


def state_kernel(bits, low, lam, q, k, v, g, out):
    head = pl.program_id(0)
    tok, width = q.shape
    out[0, 0] = mm(k[...], v[...], TN).astype(BF16)
    grad = g[...].astype(F32)
    cols = []
    for j in range(bits):
        rows = [
            grad[c * STRETCH : (c + 1) * STRETCH] * lam[head, c, low + 1 + j]
            for c in range(tok // STRETCH)
        ]
        cols.append(jnp.concatenate(rows, axis=0).astype(BF16))
    outer = mm(q[...], jnp.concatenate(cols, axis=1), TN)
    for j in range(bits):
        out[bits - j, 0] = outer[:, j * width : (j + 1) * width].astype(BF16)


def dense_kernel(lam, a, b, x, y, o1, o2, prob):
    head = pl.program_id(0)
    tok = a.shape[0]
    ri = lax.broadcasted_iota(jnp.int32, (TILE, TILE), 0)
    ci = lax.broadcasted_iota(jnp.int32, (TILE, TILE), 1)
    xor = jnp.bitwise_xor(ri, ci)
    level = jnp.zeros((TILE, TILE), jnp.int32)
    tile_levels = TILE.bit_length() - 1
    for p in range(tile_levels):
        level = level + (xor >= (1 << p)).astype(jnp.int32)
    level = jnp.where(ci <= ri, level, -1)
    big = min(256, tok)
    for r0 in range(0, tok, big):
        cols = r0 + big
        scores = mm(a[r0 : r0 + big, :], b[:cols, :], NT)
        for r in range(r0 // TILE, (r0 + big) // TILE):
            for half in range(TILE // STRETCH):
                row = r * TILE + half * STRETCH
                c = row // STRETCH
                for t in range(cols // TILE):
                    part = scores[row - r0 : row - r0 + STRETCH, t * TILE : (t + 1) * TILE]
                    if t < r:
                        part = part * lam[head, c, tile_levels + (r ^ t).bit_length()]
                    elif t == r:
                        lev = level[half * STRETCH : (half + 1) * STRETCH]
                        weight = jnp.zeros((STRETCH, TILE), F32)
                        for i in range(tile_levels + 1):
                            weight = jnp.where(lev == i, lam[head, c, i], weight)
                        part = part * weight
                    else:
                        part = jnp.zeros_like(part)
                    prob[row : row + STRETCH, t * TILE : (t + 1) * TILE] = part.astype(BF16)
        o1[r0 : r0 + big, :] = mm(prob[r0 : r0 + big, :cols], x[:cols, :], NN).astype(BF16)
    for c0 in range(0, tok, big):
        o2[c0 : c0 + big, :] = mm(prob[c0:, c0 : c0 + big], y[c0:, :], TN).astype(BF16)


def cross_kernel(bits, lam, q, k, v, g, o_in, dq_in, dk_in, dv_in, x0, rest, r0, o, dq, dk, dv):
    head = pl.program_id(0)
    tok, width = q.shape
    back = (rest[bits - 1, 0].astype(F32) + r0[0].astype(F32)).astype(BF16)
    dk[...] = (dk_in[...].astype(F32) + mm(v[...], back, NT)).astype(BF16)
    dv[...] = (dv_in[...].astype(F32) + mm(k[...], back, NN)).astype(BF16)
    states = [x0[0]] + [rest[j, 0] for j in range(bits - 1)]
    fwd = mm(q[...], jnp.concatenate(states, axis=1), NN)
    bwd = mm(g[...], jnp.concatenate(states, axis=0), NT)
    for c in range(tok // STRETCH):
        rows = slice(c * STRETCH, (c + 1) * STRETCH)
        o_sum = o_in[rows, :].astype(F32)
        q_sum = dq_in[rows, :].astype(F32)
        for j in range(bits):
            scale = lam[head, c, j]
            o_sum = o_sum + fwd[rows, j * width : (j + 1) * width] * scale
            q_sum = q_sum + bwd[rows, j * width : (j + 1) * width] * scale
        o[rows, :] = o_sum.astype(BF16)
        dq[rows, :] = q_sum.astype(BF16)


def shards(queries, keys, values, out_grad, level_table, selector):
    head_n, ctx_n = lax.axis_size("head"), lax.axis_size("ctx")
    head_i, ctx_i = lax.axis_index("head"), lax.axis_index("ctx")
    head_bits, ctx_bits = head_n.bit_length() - 1, ctx_n.bit_length() - 1
    bits = head_bits + ctx_bits
    me = ctx_i * head_n + head_i
    tok = queries.shape[0]
    heads = level_table.shape[2] * head_n
    width = queries.shape[1] // heads
    low = tok.bit_length() - 1
    stretches = tok // STRETCH

    table = lax.all_gather(level_table, "head", axis=2, tiled=True)
    mine = lax.dynamic_slice(selector, (head_i * stretches,), (stretches,))
    ids = jnp.arange(level_table.shape[0], dtype=jnp.int32)
    hot = (mine[:, None] == ids[None, :]).astype(F32)
    lev = jnp.arange(level_table.shape[1], dtype=jnp.int32).astype(F32)
    scaling = jnp.exp2(-0.5 * jnp.maximum(lev - 1.0, 0.0)) / math.sqrt(width)
    picked = jnp.sum(hot[:, :, None, None] * table[None], axis=1)
    lam = jnp.transpose(picked * scaling[None, :, None], (2, 0, 1))
    bit_ids = jnp.arange(bits, dtype=jnp.int32)
    upper = (me >> bit_ids & 1).astype(F32)
    lam_cross = lam[:, :, low + 1 : low + 1 + bits] * upper[None, None, :]

    row_spec = pl.BlockSpec((tok, width), lambda h: (0, h))
    smem = pl.BlockSpec(memory_space=pltpu.SMEM)
    row_shape = jax.ShapeDtypeStruct(queries.shape, BF16)
    params = pltpu.CompilerParams(vmem_limit_bytes=VMEM_LIMIT)
    n_bytes = tok * heads * width * 2

    packet = pl.pallas_call(
        functools.partial(state_kernel, bits, low),
        grid=(heads,),
        in_specs=[smem] + [row_spec] * 4,
        out_specs=pl.BlockSpec((bits + 1, 1, width, width), lambda h: (0, h, 0, 0)),
        out_shape=jax.ShapeDtypeStruct((bits + 1, heads, width, width), BF16),
        compiler_params=params,
        name="states",
    )(lam, queries, keys, values, out_grad)

    def dense(a, b, x, y, name):
        return pl.pallas_call(
            dense_kernel,
            grid=(heads,),
            in_specs=[smem] + [row_spec] * 4,
            out_specs=[row_spec] * 2,
            out_shape=[row_shape] * 2,
            scratch_shapes=[pltpu.VMEM((tok, tok), BF16)],
            compiler_params=params,
            cost_estimate=pl.CostEstimate(
                flops=8 * heads * tok * tok * width, bytes_accessed=6 * n_bytes, transcendentals=0
            ),
            name=name,
        )(lam, a, b, x, y)

    o_part, dv_part = dense(queries, keys, values, out_grad, "dense_out")
    dq_part, dk_part = dense(out_grad, values, keys, queries, "dense_grad")

    def swap(array, bit):
        if bit < head_bits:
            pairs = [(i, i ^ (1 << bit)) for i in range(head_n)]
            return lax.ppermute(array, "head", pairs)
        step = 1 << (bit - head_bits)
        return lax.ppermute(array, "ctx", [(i, i ^ step) for i in range(ctx_n)])

    def bit_of(bit):
        return (me >> bit & 1) == 1

    half = heads // 2
    core = head_i & 1
    got_full = swap(jnp.where(bit_of(0), packet[bits], packet[0]), 0)
    state0 = got_full
    back0 = jnp.where(bit_of(0), jnp.zeros_like(got_full), got_full)
    keep_i, send_i = core * half, (1 - core) * half
    sent = lax.dynamic_slice_in_dim(packet[:bits], send_i, half, axis=1)
    kept = lax.dynamic_slice_in_dim(packet[:bits], keep_i, half, axis=1)
    run = (kept.astype(F32) + swap(sent, 0).astype(F32)).astype(BF16)
    states = []
    back = jnp.zeros((half, width, width), F32)
    for bit in range(1, bits):
        if bit < bits - 1:
            got = swap(run, bit)
            states.append(got[0])
            back = back + jnp.where(bit_of(bit), 0.0, got[-1].astype(F32))
            run = (run[:-1].astype(F32) + got[:-1].astype(F32)).astype(BF16)
        else:
            got = swap(jnp.where(bit_of(bit), run[1], run[0]), bit)
            states.append(got)
            back = back + jnp.where(bit_of(bit), 0.0, got.astype(F32))
    ours = jnp.stack(states + [back.astype(BF16)], axis=0)
    theirs = swap(ours, 0)
    rest = jnp.where(
        core == 0,
        jnp.concatenate([ours, theirs], axis=1),
        jnp.concatenate([theirs, ours], axis=1),
    )

    mat_spec = pl.BlockSpec((1, width, width), lambda h: (h, 0, 0))
    return pl.pallas_call(
        functools.partial(cross_kernel, bits),
        grid=(heads,),
        in_specs=[smem]
        + [row_spec] * 8
        + [mat_spec, pl.BlockSpec((bits, 1, width, width), lambda h: (0, h, 0, 0)), mat_spec],
        out_specs=[row_spec] * 4,
        out_shape=[row_shape] * 4,
        compiler_params=params,
        name="cross",
    )(
        lam_cross, queries, keys, values, out_grad,
        o_part, dq_part, dk_part, dv_part, state0, rest, back0,
    )


def solution(mesh):
    rows = P(("grp", "ctx", "head"), None)
    in_specs = (rows, rows, rows, rows, P(None, None, "head"), P(("grp", "ctx")))
    return jax.shard_map(
        shards, mesh=mesh, in_specs=in_specs, out_specs=(rows,) * 4, check_vma=False
    )
```

time: 559 us -> 162 us (0.29); the launches traced: 550 us -> 161 us
  matrix products: 231 us -> 0 us
  local copies, waits for them, and re-layouts: 177 us -> 26.5 us
  Pallas kernels: 0 us -> 58.6 us
  other arithmetic: 56.1 us -> 9.78 us
  starting transfers between devices: 35.2 us -> 6.86 us
  waiting for transfers between devices: 33.6 us -> 51.9 us
  between operations: 16.2 us -> 0.84 us
  blocking collectives: 0 us -> 6.15 us
    dot_general x35 -> x0, matrix products: 231 us -> none  [the longest x4 65.2 us: shards(): jnp.einsum('thd,shd->hts', grad_block, value_part, preferred_element_type...]
    pallas_call x0 -> x4, Pallas kernels: none -> 58.6 us  [the longest x2 32.7 us: dense(): pl.pallas_call(dense_kernel, grid=(heads,), in_specs=[smem] + [row_spec]...]
    ppermute x0 -> x6, waiting for transfers between devices: none -> 51.9 us  [the longest x4 26.3 us: swap(): return lax.ppermute(array, 'head', pairs)]
    le x4 -> x0, other arithmetic: 38.2 us -> none  [shards(): col_pos[None, :] <= row_pos[:, None]]
    all_to_all x8 -> x0, starting transfers between devices: 34.7 us -> none  [the longest x1 4.92 us: shards(): lax.all_to_all(key_rows, 'head', split_axis=0, concat_axis=1, tiled=True)]
    all_to_all x8 -> x0, waiting for transfers between devices: 33.6 us -> none  [the longest x1 19.5 us: shards(): lax.all_to_all(values, 'head', split_axis=1, concat_axis=0, tiled=True)]
    all_to_all x10 -> x0, local copies, waits for them, and re-layouts: 33.2 us -> none  [the longest x2 8.23 us: shards(): lax.all_to_all(key_rows, 'head', split_axis=0, concat_axis=1, tiled=True)]
    slice x18 -> x3, local copies, waits for them, and re-layouts: 35.4 us -> 3.76 us  [the longest x2 2.3 us: shards(): states.append(got[0])]
  transfers between devices with their start and end apart: 9 -> 6, of which waited for: 5 -> 4; matrix products, arithmetic and copies ran while one was open for 56% -> 3% of each run, Pallas kernels for 0% -> 20%
where the time goes in v1:
time: 162 us; the launch traced here: 161 us
  Pallas kernels  58.6 us (36%)
  waiting for transfers between devices  51.9 us (32%)
  local copies, waits for them, and re-layouts  26.5 us (16%)
  other arithmetic  9.78 us (6%)
  starting transfers between devices  6.86 us (4%)
  blocking collectives  6.15 us (4%)
    pallas_call x2, Pallas kernels, dense(): pl.pallas_call(dense_kernel, grid=(heads,), in_specs=[smem] + [row_spec]...  32.7 us
    ppermute x4, waiting for transfers between devices, swap(): return lax.ppermute(array, 'head', pairs)  26.3 us
    ppermute x2, waiting for transfers between devices, swap(): return lax.ppermute(array, 'ctx', [(i, i ^ step) for i in range(ctx_n)])  25.6 us
    unnamed x37, local copies, waits for them, and re-layouts  19.7 us
    pallas_call x1, Pallas kernels, shards(): pl.pallas_call(functools.partial(cross_kernel, bits), grid=(heads,), in_s...  16.6 us
    pallas_call x1, Pallas kernels, shards(): pl.pallas_call(functools.partial(state_kernel, bits, low), grid=(heads,),...  9.24 us
    all_gather x1, blocking collectives, shards(): table = lax.all_gather(level_table, 'head', axis=2, tiled=True)  6.15 us
    ppermute x2, starting transfers between devices, swap(): return lax.ppermute(array, 'ctx', [(i, i ^ step) for i in range(ctx_n)])  4.42 us
  transfers between devices with their start and end apart: 6, of which 4 were waited for; matrix products, arithmetic and copies ran while one was open for 3% of the time, Pallas kernels for 20%

profile of v1, /device:TPU:0, one launch (start us, length us, event | category | flops | bytes accessed | tf_op | source)
XLA Modules:
  0.0 160.6 jit_solution(8042616211142176816)
XLA Ops:
  0.7 0.7 dynamic_slice.9
  1.4 0.1 fusion.5
  1.5 0.7 copy.13
  2.2 6.1 %all_gather.3 = f32[8,21,16]{1,0,2:T(8,128)S(1)} all-gather(f32[8,21,4]{1,0,2:T(8,128)S(1)} %copy.13), channel_id=1, replica_groups=mesh['grp'=2,'ctx'=4,'head'=4] {'head'}, dimensions={2}, use_global_device_ids=true | all-gather | bytes 13440 | tf_op jit(solution)/shard_map/all_gather | solution.py:112
  8.3 0.1 multiply_reduce_fusion
  8.5 0.0 copy-start
  8.5 1.6 copy-done
  10.1 1.6 copy-done.2
  11.7 1.6 copy-done.5
  13.3 1.6 copy-done.8
  14.9 9.2 %states.1 = bf16[5,16,128,128]{3,2,1,0:T(8,128)(2,1)S(1)} custom-call(f32[16,8,21]{2,1,0:T(8,128)S(1)} %fusion.4.lam, bf16[512,2048]{1,0:T(8,128)(2,1)S(1)} %copy-done, bf16[512,2048]{1,0:T(8,128)(2,1)S(1)} %copy-done.2, bf16[512,2048]{1,0:T(8,128)(2,1)S(1)} %copy-done.5, bf16[512,2048]{1,0:T(8,128)(2,1)S(1)} %copy-done.8), custom_call_target="tpu_custom_call" | custom-call | tf_op jit(solution)/shard_map/states/pallas_call | solution.py:130
  24.1 1.5 slice.60
  25.6 2.3 %constant_dynamic-slice_fusion = bf16[4,8,128,128]{3,2,1,0:T(8,128)(2,1)} fusion(bf16[4,16,128,128]{3,2,1,0:T(8,128)(2,1)} %slice.60, s32[]{:T(128)S(6)} %select_n.73), kind=kLoop, calls=%fused_computation.21 | loop fusion | bytes 2097156 | tf_op jit(solution)/shard_map/dynamic_slice | solution.py:174
  27.9 0.3 collective-permute-start.1
  28.2 2.7 %collective-permute-done.1 = bf16[4,8,128,128]{3,2,1,0:T(8,128)(2,1)} collective-permute-done((bf16[4,8,128,128]{3,2,1,0:T(8,128)(2,1)}, bf16[4,8,128,128]{3,2,1,0:T(8,128)(2,1)}, u32[]{:S(2)}, u32[]{:S(2)}) %collective-permute-start.1) | collective-permute-done | bytes 1048608 | tf_op jit(solution)/shard_map/ppermute | solution.py:161
  30.9 1.9 %add_convert_fusion = bf16[4,8,128,128]{3,2,1,0:T(8,128)(2,1)S(1)} fusion(bf16[4,8,128,128]{3,2,1,0:T(8,128)(2,1)} %collective-permute-done.1, bf16[4,16,128,128]{3,2,1,0:T(8,128)(2,1)} %slice.60, s32[]{:T(128)S(6)} %select_n.72), kind=kLoop, calls=%fused_computation.1 | loop fusion | flops 2097152 | bytes 3145732 | tf_op jit(solution)/shard_map/convert_element_type | solution.py:176
  32.8 2.1 %collective-permute-start.2 = (bf16[4,8,128,128]{3,2,1,0:T(8,128)(2,1)S(1)}, bf16[4,8,128,128]{3,2,1,0:T(8,128)(2,1)S(1)}, u32[]{:S(2)}, u32[]{:S(2)}) collective-permute-start(bf16[4,8,128,128]{3,2,1,0:T(8,128)(2,1)S(1)} %add_convert_fusion), channel_id=1, source_target_pairs={{0,2},{1,3},{2,0},{3,1},{4,6},{5,7},{6,4},{7,5},{8,10},{9,11},{10,... | collective-permute-start | bytes 3145736 | tf_op jit(solution)/shard_map/ppermute | solution.py:161
  34.9 23.7 %collective-permute-done.2 = bf16[4,8,128,128]{3,2,1,0:T(8,128)(2,1)S(1)} collective-permute-done((bf16[4,8,128,128]{3,2,1,0:T(8,128)(2,1)S(1)}, bf16[4,8,128,128]{3,2,1,0:T(8,128)(2,1)S(1)}, u32[]{:S(2)}, u32[]{:S(2)}) %collective-permute-start.2) | collective-permute-done | bytes 1048608 | tf_op jit(solution)/shard_map/ppermute | solution.py:161
  58.6 0.3 add_convert_fusion.1
  58.8 0.7 copy-done.17
  59.5 1.8 %collective-permute-start.3 = (bf16[3,8,128,128]{3,2,1,0:T(8,128)(2,1)S(1)}, bf16[3,8,128,128]{3,2,1,0:T(8,128)(2,1)}, u32[]{:S(2)}, u32[]{:S(2)}) collective-permute-start(bf16[3,8,128,128]{3,2,1,0:T(8,128)(2,1)S(1)} %add_convert_fusion.1), channel_id=1, source_target_pairs={{0,4},{4,0},{8,12},{12,8},{1,5},{5,1},{9,13},{13,9},{2,6},{6,2},{1... | collective-permute-start | bytes 2359304 | tf_op jit(solution)/shard_map/ppermute | solution.py:163
  61.4 17.6 %collective-permute-done.3 = bf16[3,8,128,128]{3,2,1,0:T(8,128)(2,1)} collective-permute-done((bf16[3,8,128,128]{3,2,1,0:T(8,128)(2,1)S(1)}, bf16[3,8,128,128]{3,2,1,0:T(8,128)(2,1)}, u32[]{:S(2)}, u32[]{:S(2)}) %collective-permute-start.3) | collective-permute-done | bytes 786464 | tf_op jit(solution)/shard_map/ppermute | solution.py:163
  78.9 1.2 add_convert_fusion.2
  80.2 2.6 %collective-permute-start.4 = (bf16[8,128,128]{2,1,0:T(8,128)(2,1)S(1)}, bf16[8,128,128]{2,1,0:T(8,128)(2,1)S(1)}, u32[]{:S(2)}, u32[]{:S(2)}) collective-permute-start(bf16[8,128,128]{2,1,0:T(8,128)(2,1)S(1)} %fusion.3), channel_id=1, source_target_pairs={{0,8},{4,12},{8,0},{12,4},{1,9},{5,13},{9,1},{13,5},{2,10},{6,14},... | collective-permute-start | bytes 786440 | tf_op jit(solution)/shard_map/ppermute | solution.py:163
  82.8 0.8 fusion
  83.6 1.1 slice.61
  84.7 1.2 slice.64
  85.9 0.0 copy-start.15
  85.9 8.0 %collective-permute-done.4 = bf16[8,128,128]{2,1,0:T(8,128)(2,1)S(1)} collective-permute-done((bf16[8,128,128]{2,1,0:T(8,128)(2,1)S(1)}, bf16[8,128,128]{2,1,0:T(8,128)(2,1)S(1)}, u32[]{:S(2)}, u32[]{:S(2)}) %collective-permute-start.4) | collective-permute-done | bytes 262176 | tf_op jit(solution)/shard_map/ppermute | solution.py:163
  93.9 1.2 fusion.2
  95.1 1.1 pad_maximum_fusion
  96.3 0.0 copy-start.6
  96.3 1.6 copy-done.6
  97.9 1.6 copy-done.9
  99.4 16.3 %dense_grad.1 = (bf16[512,2048]{1,0:T(8,128)(2,1)S(1)}, bf16[512,2048]{1,0:T(8,128)(2,1)S(1)}) custom-call(f32[16,8,21]{2,1,0:T(8,128)S(1)} %fusion.4.lam, bf16[512,2048]{1,0:T(8,128)(2,1)S(1)} %copy-done.9, bf16[512,2048]{1,0:T(8,128)(2,1)S(1)} %copy-done.6, bf16[512,2048]{1,0:T(8,128)(2,1)S(1)} %copy-done.3, bf16[512,2048]{1,0:T(8,128)(2,1)S(1)} %copy-done.1), custom_call_target="tpu_custom_call" | custom-call | flops 4294967296 | bytes 12582912 | tf_op jit(solution)/shard_map/dense_grad/pallas_call | solution.py:141
  115.8 0.0 copy-start.11
  115.8 1.3 copy-done.11
  117.1 1.3 copy-done.13
  118.4 0.1 slice_multiply_fusion.lam
  118.5 0.0 copy-start.4
  118.5 1.6 copy-done.4
  120.1 1.6 copy-done.7
  121.7 1.6 copy-done.10
  123.3 16.3 %dense_out.1 = (bf16[512,2048]{1,0:T(8,128)(2,1)S(1)}, bf16[512,2048]{1,0:T(8,128)(2,1)S(1)}) custom-call(f32[16,8,21]{2,1,0:T(8,128)S(1)} %fusion.4.lam, bf16[512,2048]{1,0:T(8,128)(2,1)S(1)} %copy-done.1, bf16[512,2048]{1,0:T(8,128)(2,1)S(1)} %copy-done.4, bf16[512,2048]{1,0:T(8,128)(2,1)S(1)} %copy-done.7, bf16[512,2048]{1,0:T(8,128)(2,1)S(1)} %copy-done.10), custom_call_target="tpu_custom_call" | custom-call | flops 4294967296 | bytes 12582912 | tf_op jit(solution)/shard_map/dense_out/pallas_call | solution.py:141
  139.7 1.3 copy-done.14
  141.0 0.0 copy-start.12
  141.0 2.9 %maximum_select_fusion.rest = bf16[4,16,128,128]{3,2,1,0:T(8,128)(2,1)} fusion(bf16[4,8,128,128]{3,2,1,0:T(8,128)(2,1)} %collective-permute-done.5, bf16[1,8,128,128]{3,2,1,0:T(8,128)(2,1)S(1)} %fusion.2, bf16[1,8,128,128]{3,2,1,0:T(8,128)(2,1)S(1)} %bitcast.16, bf16[1,8,128,128]{3,2,1,0:T(8,128)(2,1)S(1)} %copy-done.16, ...), kind=kLoop, calls=%fused_computation | loop fusion | flops 9437184 | bytes 4194305 | tf_op jit(solution)/shard_map/jit(_where)/select_n | solution.py:191
  143.9 16.6 %cross.1 = (bf16[512,2048]{1,0:T(8,128)(2,1)}, bf16[512,2048]{1,0:T(8,128)(2,1)}, bf16[512,2048]{1,0:T(8,128)(2,1)}, bf16[512,2048]{1,0:T(8,128)(2,1)}) custom-call(f32[16,8,4]{2,1,0:T(8,128)S(1)} %slice_multiply_fusion.lam, bf16[512,2048]{1,0:T(8,128)(2,1)S(1)} %copy-done.1, bf16[512,2048]{1,0:T(8,128)(2,1)S(1)} %copy-done.4, ...), custom_call_target="tpu_custom_call" | custom-call | tf_op jit(solution)/shard_map/cross/pallas_call | solution.py:198
  (27 shorter events, 0.2 us)
Async XLA Ops:
  8.5 1.6 copy-start
  10.1 1.6 copy-start.2
  11.7 1.6 copy-start.5
  13.3 1.6 copy-start.8
  27.9 3.0 %collective-permute-start.1 = (bf16[4,8,128,128]{3,2,1,0:T(8,128)(2,1)}, bf16[4,8,128,128]{3,2,1,0:T(8,128)(2,1)}, u32[]{:S(2)}, u32[]{:S(2)}) collective-permute-start(bf16[4,8,128,128]{3,2,1,0:T(8,128)(2,1)} %constant_dynamic-slice_fusion), channel_id=1, source_target_pairs={{0,1},{1,0},{2,3},{3,2},{4,5},{5,4},{6,7},{7,6},{8,9},{9,8},{10,11... | collective-permute-start | bytes 3145736 | tf_op jit(solution)/shard_map/ppermute | solution.py:161
  32.8 25.8 %collective-permute-start.2 = (bf16[4,8,128,128]{3,2,1,0:T(8,128)(2,1)S(1)}, bf16[4,8,128,128]{3,2,1,0:T(8,128)(2,1)S(1)}, u32[]{:S(2)}, u32[]{:S(2)}) collective-permute-start(bf16[4,8,128,128]{3,2,1,0:T(8,128)(2,1)S(1)} %add_convert_fusion), channel_id=1, source_target_pairs={{0,2},{1,3},{2,0},{3,1},{4,6},{5,7},{6,4},{7,5},{8,10},{9,11},{10,... | collective-permute-start | bytes 3145736 | tf_op jit(solution)/shard_map/ppermute | solution.py:161
  58.6 1.0 copy-start.17
  59.5 19.4 %collective-permute-start.3 = (bf16[3,8,128,128]{3,2,1,0:T(8,128)(2,1)S(1)}, bf16[3,8,128,128]{3,2,1,0:T(8,128)(2,1)}, u32[]{:S(2)}, u32[]{:S(2)}) collective-permute-start(bf16[3,8,128,128]{3,2,1,0:T(8,128)(2,1)S(1)} %add_convert_fusion.1), channel_id=1, source_target_pairs={{0,4},{4,0},{8,12},{12,8},{1,5},{5,1},{9,13},{13,9},{2,6},{6,2},{1... | collective-permute-start | bytes 2359304 | tf_op jit(solution)/shard_map/ppermute | solution.py:163
  80.2 13.8 %collective-permute-start.4 = (bf16[8,128,128]{2,1,0:T(8,128)(2,1)S(1)}, bf16[8,128,128]{2,1,0:T(8,128)(2,1)S(1)}, u32[]{:S(2)}, u32[]{:S(2)}) collective-permute-start(bf16[8,128,128]{2,1,0:T(8,128)(2,1)S(1)} %fusion.3), channel_id=1, source_target_pairs={{0,8},{4,12},{8,0},{12,4},{1,9},{5,13},{9,1},{13,5},{2,10},{6,14},... | collective-permute-start | bytes 786440 | tf_op jit(solution)/shard_map/ppermute | solution.py:163
  83.6 57.3 %collective-permute-start = (bf16[16,128,128]{2,1,0:T(8,128)(2,1)}, bf16[16,128,128]{2,1,0:T(8,128)(2,1)S(1)}, u32[]{:S(2)}, u32[]{:S(2)}) collective-permute-start(bf16[16,128,128]{2,1,0:T(8,128)(2,1)} %fusion), channel_id=1, source_target_pairs={{0,1},{1,0},{2,3},{3,2},{4,5},{5,4},{6,7},{7,6},{8,9},{9,8},{10,11... | collective-permute-start | bytes 1572872 | tf_op jit(solution)/shard_map/ppermute | solution.py:161
  83.6 12.6 %copy-start.1 = (bf16[512,2048]{1,0:T(8,128)(2,1)S(1)}, bf16[512,2048]{1,0:T(8,128)(2,1)}, u32[]{:S(2)}) copy-start(bf16[512,2048]{1,0:T(8,128)(2,1)} %q.3) | copy-start | bytes 6291460
  83.6 12.6 %copy-start.3 = (bf16[512,2048]{1,0:T(8,128)(2,1)S(1)}, bf16[512,2048]{1,0:T(8,128)(2,1)}, u32[]{:S(2)}) copy-start(bf16[512,2048]{1,0:T(8,128)(2,1)} %k.3) | copy-start | bytes 6291460
  85.9 10.3 %copy-start.15 = (bf16[1,8,128,128]{3,2,1,0:T(8,128)(2,1)}, bf16[1,8,128,128]{3,2,1,0:T(8,128)(2,1)S(1)}, u32[]{:S(2)}) copy-start(bf16[1,8,128,128]{3,2,1,0:T(8,128)(2,1)S(1)} %slice.64) | copy-start | bytes 786436
  96.2 44.8 %collective-permute-start.5 = (bf16[4,8,128,128]{3,2,1,0:T(8,128)(2,1)}, bf16[4,8,128,128]{3,2,1,0:T(8,128)(2,1)}, u32[]{:S(2)}, u32[]{:S(2)}) collective-permute-start(bf16[4,8,128,128]{3,2,1,0:T(8,128)(2,1)} %pad_maximum_fusion), channel_id=1, source_target_pairs={{0,1},{1,0},{2,3},{3,2},{4,5},{5,4},{6,7},{7,6},{8,9},{9,8},{10,11... | collective-permute-start | bytes 3145736 | tf_op jit(solution)/shard_map/ppermute | solution.py:161
  96.3 1.6 copy-start.6
  97.9 1.6 copy-start.9
  115.8 1.3 copy-start.11
  117.1 1.3 copy-start.13
  118.5 1.6 copy-start.4
  120.1 1.6 copy-start.7
  121.7 1.6 copy-start.10
  123.3 17.7 %copy-start.16 = (bf16[1,8,128,128]{3,2,1,0:T(8,128)(2,1)S(1)}, bf16[1,8,128,128]{3,2,1,0:T(8,128)(2,1)}, u32[]{:S(2)}) copy-start(bf16[1,8,128,128]{3,2,1,0:T(8,128)(2,1)} %copy-done.15) | copy-start | bytes 786436
  139.7 1.3 copy-start.14
  141.0 2.9 %copy-start.12 = (bf16[512,2048]{1,0:T(8,128)(2,1)S(1)}, bf16[512,2048]{1,0:T(8,128)(2,1)}, u32[]{:S(2)}) copy-start(bf16[512,2048]{1,0:T(8,128)(2,1)} %copy-done.11) | copy-start | bytes 6291460

commit v2 on v1

v2 whole, which is shorter than its diff:
```python
import functools
import math

import jax
import jax.numpy as jnp
from jax import lax
from jax.experimental import pallas as pl
from jax.experimental.pallas import tpu as pltpu
from jax.sharding import PartitionSpec as P

F32 = jnp.float32
BF16 = jnp.bfloat16
STRETCH = 64
TILE = 128
NT = (((1,), (1,)), ((), ()))
TN = (((0,), (0,)), ((), ()))
NN = (((1,), (0,)), ((), ()))
VMEM_LIMIT = 62 * 1024 * 1024
GROUP = 2


def mm(a, b, dims):
    return lax.dot_general(a, b, dims, preferred_element_type=F32)


def state_kernel(bits, low, lam, q_all, k_all, v_all, g_all, out):
    tok = q_all.shape[0]
    width = q_all.shape[1] // GROUP
    for n in range(GROUP):
        head = pl.program_id(0) * GROUP + n
        lanes = slice(n * width, (n + 1) * width)
        q, k, v = q_all[:, lanes], k_all[:, lanes], v_all[:, lanes]
        grad = g_all[:, lanes].astype(F32)
        out[0, n] = mm(k, v, TN).astype(BF16)
        cols = []
        for j in range(bits):
            rows = [
                grad[c * STRETCH : (c + 1) * STRETCH] * lam[head, c, low + 1 + j]
                for c in range(tok // STRETCH)
            ]
            cols.append(jnp.concatenate(rows, axis=0).astype(BF16))
        outer = mm(q, jnp.concatenate(cols, axis=1), TN)
        for j in range(bits):
            out[bits - j, n] = outer[:, j * width : (j + 1) * width].astype(BF16)


def dense_kernel(lam, a, b, x, y, after, o1, o2, token, prob):
    del after
    tok = a.shape[0]
    width = a.shape[1] // GROUP
    token[...] = jnp.zeros_like(token)
    ri = lax.broadcasted_iota(jnp.int32, (TILE, TILE), 0)
    ci = lax.broadcasted_iota(jnp.int32, (TILE, TILE), 1)
    xor = jnp.bitwise_xor(ri, ci)
    level = jnp.zeros((TILE, TILE), jnp.int32)
    tile_levels = TILE.bit_length() - 1
    for p in range(tile_levels):
        level = level + (xor >= (1 << p)).astype(jnp.int32)
    level = jnp.where(ci <= ri, level, -1)
    big = min(256, tok)
    for n in range(GROUP):
        head = pl.program_id(0) * GROUP + n
        lanes = slice(n * width, (n + 1) * width)
        for r0 in range(0, tok, big):
            cols = r0 + big
            scores = mm(a[r0 : r0 + big, lanes], b[:cols, lanes], NT)
            for r in range(r0 // TILE, (r0 + big) // TILE):
                for half in range(TILE // STRETCH):
                    row = r * TILE + half * STRETCH
                    c = row // STRETCH
                    for t in range(cols // TILE):
                        part = scores[row - r0 : row - r0 + STRETCH, t * TILE : (t + 1) * TILE]
                        if t < r:
                            part = part * lam[head, c, tile_levels + (r ^ t).bit_length()]
                        elif t == r:
                            lev = level[half * STRETCH : (half + 1) * STRETCH]
                            weight = jnp.zeros((STRETCH, TILE), F32)
                            for i in range(tile_levels + 1):
                                weight = jnp.where(lev == i, lam[head, c, i], weight)
                            part = part * weight
                        else:
                            part = jnp.zeros_like(part)
                        prob[n, row : row + STRETCH, t * TILE : (t + 1) * TILE] = part.astype(BF16)
            o1[r0 : r0 + big, lanes] = mm(
                prob[n, r0 : r0 + big, :cols], x[:cols, lanes], NN
            ).astype(BF16)
        for c0 in range(0, tok, big):
            o2[c0 : c0 + big, lanes] = mm(
                prob[n, c0:, c0 : c0 + big], y[c0:, lanes], TN
            ).astype(BF16)


def cross_kernel(
    bits, lam, pick, q, k, v, g, o_in, dq_in, dk_in, dv_in, x0, ours, theirs, r0, o, dq, dk, dv
):
    tok = q.shape[0]
    width = q.shape[1] // GROUP
    own = pick[pl.program_id(0)] == 1
    for n in range(GROUP):
        head = pl.program_id(0) * GROUP + n
        lanes = slice(n * width, (n + 1) * width)
        rest = [jnp.where(own, ours[j, n], theirs[j, n]) for j in range(bits)]
        back = (rest[bits - 1].astype(F32) + r0[n].astype(F32)).astype(BF16)
        dk[:, lanes] = (dk_in[:, lanes].astype(F32) + mm(v[:, lanes], back, NT)).astype(BF16)
        dv[:, lanes] = (dv_in[:, lanes].astype(F32) + mm(k[:, lanes], back, NN)).astype(BF16)
        states = [x0[n]] + rest[: bits - 1]
        fwd = mm(q[:, lanes], jnp.concatenate(states, axis=1), NN)
        bwd = mm(g[:, lanes], jnp.concatenate(states, axis=0), NT)
        for c in range(tok // STRETCH):
            rows = slice(c * STRETCH, (c + 1) * STRETCH)
            o_sum = o_in[rows, lanes].astype(F32)
            q_sum = dq_in[rows, lanes].astype(F32)
            for j in range(bits):
                scale = lam[head, c, j]
                o_sum = o_sum + fwd[rows, j * width : (j + 1) * width] * scale
                q_sum = q_sum + bwd[rows, j * width : (j + 1) * width] * scale
            o[rows, lanes] = o_sum.astype(BF16)
            dq[rows, lanes] = q_sum.astype(BF16)


def shards(queries, keys, values, out_grad, level_table, selector):
    head_n, ctx_n = lax.axis_size("head"), lax.axis_size("ctx")
    head_i, ctx_i = lax.axis_index("head"), lax.axis_index("ctx")
    head_bits, ctx_bits = head_n.bit_length() - 1, ctx_n.bit_length() - 1
    bits = head_bits + ctx_bits
    me = ctx_i * head_n + head_i
    tok = queries.shape[0]
    heads = level_table.shape[2] * head_n
    width = queries.shape[1] // heads
    low = tok.bit_length() - 1
    stretches = tok // STRETCH

    table = lax.all_gather(level_table, "head", axis=2, tiled=True)
    mine = lax.dynamic_slice(selector, (head_i * stretches,), (stretches,))
    ids = jnp.arange(level_table.shape[0], dtype=jnp.int32)
    hot = (mine[:, None] == ids[None, :]).astype(F32)
    lev = jnp.arange(level_table.shape[1], dtype=jnp.int32).astype(F32)
    scaling = jnp.exp2(-0.5 * jnp.maximum(lev - 1.0, 0.0)) / math.sqrt(width)
    picked = jnp.sum(hot[:, :, None, None] * table[None], axis=1)
    lam = jnp.transpose(picked * scaling[None, :, None], (2, 0, 1))
    bit_ids = jnp.arange(bits, dtype=jnp.int32)
    upper = (me >> bit_ids & 1).astype(F32)
    lam_cross = lam[:, :, low + 1 : low + 1 + bits] * upper[None, None, :]

    row_spec = pl.BlockSpec((tok, GROUP * width), lambda h: (0, h))
    smem = pl.BlockSpec(memory_space=pltpu.SMEM)
    row_shape = jax.ShapeDtypeStruct(queries.shape, BF16)
    params = pltpu.CompilerParams(vmem_limit_bytes=VMEM_LIMIT)
    n_bytes = tok * heads * width * 2

    packet = pl.pallas_call(
        functools.partial(state_kernel, bits, low),
        grid=(heads // GROUP,),
        in_specs=[smem] + [row_spec] * 4,
        out_specs=pl.BlockSpec((bits + 1, GROUP, width, width), lambda h: (0, h, 0, 0)),
        out_shape=jax.ShapeDtypeStruct((bits + 1, heads, width, width), BF16),
        compiler_params=params,
        name="states",
    )(lam, queries, keys, values, out_grad)

    def dense(a, b, x, y, after, name):
        return pl.pallas_call(
            dense_kernel,
            grid=(heads // GROUP,),
            in_specs=[smem] + [row_spec] * 4 + [pl.BlockSpec(memory_space=pl.ANY)],
            out_specs=[row_spec] * 2 + [pl.BlockSpec((8, 128), lambda h: (0, 0))],
            out_shape=[row_shape] * 2 + [jax.ShapeDtypeStruct((8, 128), F32)],
            scratch_shapes=[pltpu.VMEM((GROUP, tok, tok), BF16)],
            compiler_params=params,
            cost_estimate=pl.CostEstimate(
                flops=8 * heads * tok * tok * width, bytes_accessed=6 * n_bytes, transcendentals=0
            ),
            name=name,
        )(lam, a, b, x, y, after)

    def swap(array, bit):
        if bit < head_bits:
            pairs = [(i, i ^ (1 << bit)) for i in range(head_n)]
            return lax.ppermute(array, "head", pairs)
        step = 1 << (bit - head_bits)
        return lax.ppermute(array, "ctx", [(i, i ^ step) for i in range(ctx_n)])

    def bit_of(bit):
        return (me >> bit & 1) == 1

    half = heads // 2
    core = head_i & 1
    got_full = swap(jnp.where(bit_of(0), packet[bits], packet[0]), 0)
    state0 = got_full
    back0 = jnp.where(bit_of(0), jnp.zeros_like(got_full), got_full)
    keep_i, send_i = core * half, (1 - core) * half
    sent = lax.dynamic_slice_in_dim(packet[:bits], send_i, half, axis=1)
    kept = lax.dynamic_slice_in_dim(packet[:bits], keep_i, half, axis=1)
    run = (kept.astype(F32) + swap(sent, 0).astype(F32)).astype(BF16)
    states = []
    back = jnp.zeros((half, width, width), F32)
    work = [
        (queries, keys, values, out_grad, "dense_out"),
        (out_grad, values, keys, queries, "dense_grad"),
    ]
    parts = []
    for bit in range(1, bits):
        last = bit == bits - 1
        sent = jnp.where(bit_of(bit), run[1], run[0]) if last else run
        got = swap(sent, bit).astype(F32)
        while work and (len(parts) < bit or last):
            *arrays, name = work.pop(0)
            first, second, token = dense(*arrays, sent, name)
            parts += [(first, second)]
            got = got + token[0, 0]
        if last:
            states.append(got.astype(BF16))
            back = back + jnp.where(bit_of(bit), 0.0, got)
        else:
            states.append(got[0].astype(BF16))
            back = back + jnp.where(bit_of(bit), 0.0, got[-1])
            run = (run[:-1].astype(F32) + got[:-1]).astype(BF16)
    (o_part, dv_part), (dq_part, dk_part) = parts
    ours = jnp.stack(states + [back.astype(BF16)], axis=0)
    theirs = swap(ours, 0)
    steps = half // GROUP
    pick = (jnp.arange(heads // GROUP, dtype=jnp.int32) // steps == core).astype(jnp.int32)

    mat_spec = pl.BlockSpec((GROUP, width, width), lambda h: (h, 0, 0))
    half_spec = pl.BlockSpec((bits, GROUP, width, width), lambda h: (0, h % steps, 0, 0))
    return pl.pallas_call(
        functools.partial(cross_kernel, bits),
        grid=(heads // GROUP,),
        in_specs=[smem] * 2 + [row_spec] * 8 + [mat_spec, half_spec, half_spec, mat_spec],
        out_specs=[row_spec] * 4,
        out_shape=[row_shape] * 4,
        compiler_params=params,
        name="cross",
    )(
        lam_cross, pick, queries, keys, values, out_grad,
        o_part, dq_part, dk_part, dv_part, state0, ours, theirs, back0,
    )


def solution(mesh):
    rows = P(("grp", "ctx", "head"), None)
    in_specs = (rows, rows, rows, rows, P(None, None, "head"), P(("grp", "ctx")))
    return jax.shard_map(
        shards, mesh=mesh, in_specs=in_specs, out_specs=(rows,) * 4, check_vma=False
    )
```

time: 162 us -> 111 us (0.69)
  waiting for transfers between devices: 51.9 us -> 25.1 us
  local copies, waits for them, and re-layouts: 26.5 us -> 9.37 us
  Pallas kernels: 58.6 us -> 50 us
    unnamed x37 -> x19, local copies, waits for them, and re-layouts: 19.7 us -> 3.05 us
    ppermute x4, waiting for transfers between devices: 26.3 us -> 12.2 us  [swap(): return lax.ppermute(array, 'head', pairs)]
    ppermute x2, waiting for transfers between devices: 25.6 us -> 12.9 us  [swap(): return lax.ppermute(array, 'ctx', [(i, i ^ step) for i in range(ctx_n)])]
    pallas_call x4, Pallas kernels: 58.6 us -> 50 us  [the longest x2 26.5 us: dense(): pl.pallas_call(dense_kernel, grid=(heads // GROUP,), in_specs=[smem] + [r...]
    add x0 -> x2, other arithmetic: none -> 2.96 us  [shards(): got = got + token[0, 0]]
    select_n x2 -> x1, other arithmetic: 2.94 us -> 0.03 us  [shards(): sent = jnp.where(bit_of(bit), run[1], run[0]) if last else run]
    dynamic_slice x1, local copies, waits for them, and re-layouts: 2.31 us -> 0.11 us  [shards(): sent = lax.dynamic_slice_in_dim(packet[:bits], send_i, half, axis=1)]
    slice x2 -> x4, local copies, waits for them, and re-layouts: 2.3 us -> 3.74 us  [the longest x2 2.62 us: shards(): got = got + token[0, 0]]
  transfers between devices with their start and end apart: 6 -> 6, of which waited for: 4 -> 5; matrix products, arithmetic and copies ran while one was open for 3% -> 7% of each run, Pallas kernels for 20% -> 24%
where the time goes in v2:
time: 111 us; the launch traced here: 109 us
  Pallas kernels  50 us (45%)
  waiting for transfers between devices  25.1 us (23%)
  other arithmetic  10.8 us (10%)
  local copies, waits for them, and re-layouts  9.37 us (8%)
  starting transfers between devices  7.29 us (7%)
  blocking collectives  6.15 us (6%)
    pallas_call x2, Pallas kernels, dense(): pl.pallas_call(dense_kernel, grid=(heads // GROUP,), in_specs=[smem] + [r...  26.5 us
    pallas_call x1, Pallas kernels, shards(): pl.pallas_call(functools.partial(cross_kernel, bits), grid=(heads // GROU...  14.3 us
    ppermute x2, waiting for transfers between devices, swap(): return lax.ppermute(array, 'ctx', [(i, i ^ step) for i in range(ctx_n)])  12.9 us
    ppermute x4, waiting for transfers between devices, swap(): return lax.ppermute(array, 'head', pairs)  12.2 us
    pallas_call x1, Pallas kernels, shards(): pl.pallas_call(functools.partial(state_kernel, bits, low), grid=(heads //...  9.21 us
    all_gather x1, blocking collectives, shards(): table = lax.all_gather(level_table, 'head', axis=2, tiled=True)  6.15 us
    ppermute x2, starting transfers between devices, swap(): return lax.ppermute(array, 'ctx', [(i, i ^ step) for i in range(ctx_n)])  4.47 us
    unnamed x19, local copies, waits for them, and re-layouts  3.05 us
  transfers between devices with their start and end apart: 6, of which 5 were waited for; matrix products, arithmetic and copies ran while one was open for 7% of the time, Pallas kernels for 24%

profile of v2, /device:TPU:0, one launch (start us, length us, event | category | flops | bytes accessed | tf_op | source)
XLA Modules:
  0.0 109.5 jit_solution(1227409896087174721)
XLA Ops:
  0.7 0.7 dynamic_slice.9
  1.4 0.1 fusion.10
  1.5 0.7 copy.13
  2.2 6.1 %all_gather.3 = f32[8,21,16]{1,0,2:T(8,128)S(1)} all-gather(f32[8,21,4]{1,0,2:T(8,128)S(1)} %copy.13), channel_id=1, replica_groups=mesh['grp'=2,'ctx'=4,'head'=4] {'head'}, dimensions={2}, use_global_device_ids=true | all-gather | bytes 13440 | tf_op jit(solution)/shard_map/all_gather | solution.py:133
  8.3 0.1 multiply_reduce_fusion
  8.5 0.7 fusion.9.lam
  9.1 9.2 %states.1 = bf16[5,16,128,128]{3,2,1,0:T(8,128)(2,1)} custom-call(f32[16,8,21]{2,1,0:T(8,128)} %fusion.9.lam, bf16[512,2048]{1,0:T(8,128)(2,1)} %q.1, bf16[512,2048]{1,0:T(8,128)(2,1)} %k.1, bf16[512,2048]{1,0:T(8,128)(2,1)} %v.1, bf16[512,2048]{1,0:T(8,128)(2,1)} %g.1), custom_call_target="tpu_custom_call" | custom-call | tf_op jit(solution)/shard_map/states/pallas_call | solution.py:151
  18.3 1.7 %slice.68 = bf16[4,16,128,128]{3,2,1,0:T(8,128)(2,1)S(1)} slice(bf16[5,16,128,128]{3,2,1,0:T(8,128)(2,1)} %states.1), slice={[0:4], [0:16], [0:128], [0:128]} | slice | bytes 4194304 | tf_op jit(solution)/shard_map/slice | solution.py:193
  20.1 0.1 constant_dynamic-slice_fusion
  20.2 0.4 collective-permute-start
  20.6 2.5 %collective-permute-done = bf16[4,8,128,128]{3,2,1,0:T(8,128)(2,1)} collective-permute-done((bf16[4,8,128,128]{3,2,1,0:T(8,128)(2,1)S(1)}, bf16[4,8,128,128]{3,2,1,0:T(8,128)(2,1)}, u32[]{:S(2)}, u32[]{:S(2)}) %collective-permute-start) | collective-permute-done | bytes 1048608 | tf_op jit(solution)/shard_map/ppermute | solution.py:179
  23.1 1.6 %add_convert_fusion.after = bf16[4,8,128,128]{3,2,1,0:T(8,128)(2,1)S(1)} fusion(bf16[4,8,128,128]{3,2,1,0:T(8,128)(2,1)} %collective-permute-done, bf16[4,16,128,128]{3,2,1,0:T(8,128)(2,1)S(1)} %slice.68, s32[]{:T(128)S(6)} %select_n.66), kind=kLoop, calls=%fused_computation.1 | loop fusion | flops 2097152 | bytes 3145732 | tf_op jit(solution)/shard_map/convert_element_type | solution.py:194
  24.6 0.0 copy-start.2
  24.7 2.1 %collective-permute-start.1 = (bf16[4,8,128,128]{3,2,1,0:T(8,128)(2,1)S(1)}, bf16[4,8,128,128]{3,2,1,0:T(8,128)(2,1)}, u32[]{:S(2)}, u32[]{:S(2)}) collective-permute-start(bf16[4,8,128,128]{3,2,1,0:T(8,128)(2,1)S(1)} %add_convert_fusion.after), channel_id=1, source_target_pairs={{0,2},{1,3},{2,0},{3,1},{4,6},{5,7},{6,4},{7,5},{8,10},{9,11},{10,... | collective-permute-start | bytes 3145736 | tf_op jit(solution)/shard_map/ppermute | solution.py:179
  26.7 0.0 copy-done.2
  26.8 13.2 %dense_out.1 = (bf16[512,2048]{1,0:T(8,128)(2,1)}, bf16[512,2048]{1,0:T(8,128)(2,1)}, f32[8,128]{1,0:T(8,128)}) custom-call(f32[16,8,21]{2,1,0:T(8,128)} %fusion.9.lam, bf16[512,2048]{1,0:T(8,128)(2,1)} %q.1, bf16[512,2048]{1,0:T(8,128)(2,1)} %k.1, bf16[512,2048]{1,0:T(8,128)(2,1)} %v.1, bf16[512,2048]{1,0:T(8,128)(2,1)} %g.1, bf16[4,8,128,128]{3,2,1,0:T(8,128)(2,1)} %copy-done.2), custom_call_target="tpu_custom_call" | custom-call | flops 4294967296 | bytes 12582912 | tf_op jit(solution)/shard_map/dense_out/pallas_call | solution.py:162
  40.0 1.3 %slice.54 = f32[1,1]{1,0:T(1,128)} slice(f32[8,128]{1,0:T(8,128)} %get-tuple-element.11), slice={[0:1], [0:1]} | slice | bytes 8 | tf_op jit(solution)/shard_map/slice | solution.py:210
  41.3 9.2 %collective-permute-done.1 = bf16[4,8,128,128]{3,2,1,0:T(8,128)(2,1)} collective-permute-done((bf16[4,8,128,128]{3,2,1,0:T(8,128)(2,1)S(1)}, bf16[4,8,128,128]{3,2,1,0:T(8,128)(2,1)}, u32[]{:S(2)}, u32[]{:S(2)}) %collective-permute-start.1) | collective-permute-done | bytes 1048608 | tf_op jit(solution)/shard_map/ppermute | solution.py:179
  50.5 2.1 %convert_add_fusion = f32[4,8,128,128]{3,2,1,0:T(8,128)S(1)} fusion(bf16[4,8,128,128]{3,2,1,0:T(8,128)(2,1)} %collective-permute-done.1, f32[]{:T(128)} %bitcast.1), kind=kLoop, calls=%fused_computation | loop fusion | flops 1048576 | bytes 3145732 | tf_op jit(solution)/shard_map/add | solution.py:210
  52.6 0.0 copy-start
  52.6 1.3 %copy-done = f32[4,8,128,128]{3,2,1,0:T(8,128)} copy-done((f32[4,8,128,128]{3,2,1,0:T(8,128)}, f32[4,8,128,128]{3,2,1,0:T(8,128)S(1)}, u32[]{:S(2)}) %copy-start) | copy-done | bytes 2097176
  54.0 0.0 copy-done.3
  54.0 0.2 fusion.after
  54.2 0.0 copy-start.4
  54.2 1.9 %collective-permute-start.3 = (bf16[3,8,128,128]{3,2,1,0:T(8,128)(2,1)S(1)}, bf16[3,8,128,128]{3,2,1,0:T(8,128)(2,1)S(1)}, u32[]{:S(2)}, u32[]{:S(2)}) collective-permute-start(bf16[3,8,128,128]{3,2,1,0:T(8,128)(2,1)S(1)} %fusion.after), channel_id=1, source_target_pairs={{0,4},{4,0},{8,12},{12,8},{1,5},{5,1},{9,13},{13,9},{2,6},{6,2},{1... | collective-permute-start | bytes 2359304 | tf_op jit(solution)/shard_map/ppermute | solution.py:181
  56.1 0.0 copy-done.4
  56.1 13.3 %dense_grad.1 = (bf16[512,2048]{1,0:T(8,128)(2,1)}, bf16[512,2048]{1,0:T(8,128)(2,1)}, f32[8,128]{1,0:T(8,128)}) custom-call(f32[16,8,21]{2,1,0:T(8,128)} %fusion.9.lam, bf16[512,2048]{1,0:T(8,128)(2,1)} %g.1, bf16[512,2048]{1,0:T(8,128)(2,1)} %v.1, bf16[512,2048]{1,0:T(8,128)(2,1)} %k.1, bf16[512,2048]{1,0:T(8,128)(2,1)} %q.1, ...), custom_call_target="tpu_custom_call" | custom-call | flops 4294967296 | bytes 12582912 | tf_op jit(solution)/shard_map/dense_grad/pallas_call | solution.py:162
  69.4 1.3 %slice.59 = f32[1,1]{1,0:T(1,128)} slice(f32[8,128]{1,0:T(8,128)} %get-tuple-element.15), slice={[0:1], [0:1]} | slice | bytes 8 | tf_op jit(solution)/shard_map/slice | solution.py:210
  70.7 2.9 %collective-permute-done.3 = bf16[3,8,128,128]{3,2,1,0:T(8,128)(2,1)S(1)} collective-permute-done((bf16[3,8,128,128]{3,2,1,0:T(8,128)(2,1)S(1)}, bf16[3,8,128,128]{3,2,1,0:T(8,128)(2,1)S(1)}, u32[]{:S(2)}, u32[]{:S(2)}) %collective-permute-start.3) | collective-permute-done | bytes 786464 | tf_op jit(solution)/shard_map/ppermute | solution.py:181
  73.5 0.8 convert_add_fusion.1
  74.4 0.0 copy-done.5
  74.4 0.1 fusion.1
  74.6 2.6 %collective-permute-start.4 = (bf16[8,128,128]{2,1,0:T(8,128)(2,1)S(1)}, bf16[8,128,128]{2,1,0:T(8,128)(2,1)S(1)}, u32[]{:S(2)}, u32[]{:S(2)}) collective-permute-start(bf16[8,128,128]{2,1,0:T(8,128)(2,1)S(1)} %fusion.8), channel_id=1, source_target_pairs={{0,8},{4,12},{8,0},{12,4},{1,9},{5,13},{9,1},{13,5},{2,10},{6,14},... | collective-permute-start | bytes 786440 | tf_op jit(solution)/shard_map/ppermute | solution.py:181
  77.2 1.1 slice.117
  78.3 10.1 %collective-permute-done.4 = bf16[8,128,128]{2,1,0:T(8,128)(2,1)S(1)} collective-permute-done((bf16[8,128,128]{2,1,0:T(8,128)(2,1)S(1)}, bf16[8,128,128]{2,1,0:T(8,128)(2,1)S(1)}, u32[]{:S(2)}, u32[]{:S(2)}) %collective-permute-start.4) | collective-permute-done | bytes 262176 | tf_op jit(solution)/shard_map/ppermute | solution.py:181
  88.4 1.2 %fusion.7 = bf16[1,8,128,128]{3,2,1,0:T(8,128)(2,1)S(1)} fusion(bf16[8,128,128]{2,1,0:T(8,128)(2,1)S(1)} %collective-permute-done.4, f32[3,8,128,128]{3,2,1,0:T(8,128)S(1)} %convert_add_fusion.1, f32[4,8,128,128]{3,2,1,0:T(8,128)} %copy-done, pred[]{:T(512)S(6)} %eq.43, pred[]{:T(512)S(6)} %eq.45, pred[]{:T(512)S(6)} %eq.44), kind=kLoop, calls=%fused_computation.20 | loop fusion | flops 917504 | bytes 1572867 | tf_op jit(solution)/shard_map/stack | solution.py:219
  89.5 0.0 copy-start.8
  89.5 0.1 pad_maximum_fusion.ours
  89.7 0.1 collective-permute-start.5
  89.8 1.6 %fusion.6 = bf16[16,128,128]{2,1,0:T(8,128)(2,1)S(1)} fusion(bf16[5,16,128,128]{3,2,1,0:T(8,128)(2,1)} %states.1, pred[]{:T(512)S(6)} %eq.42), kind=kLoop, calls=%fused_computation.17 | loop fusion | flops 262144 | bytes 1572865 | tf_op jit(solution)/shard_map/jit(_where)/select_n | solution.py:188
  91.3 0.3 collective-permute-start.2
  91.6 0.5 compare_convert_fusion.pick
  92.1 0.7 slice_multiply_fusion.lam
  92.8 0.5 collective-permute-done.2.x0
  93.3 0.9 broadcast_select_fusion.r0
  94.2 0.0 collective-permute-done.5.theirs
  94.2 1.0 copy-done.7
  95.2 14.3 %cross.1 = (bf16[512,2048]{1,0:T(8,128)(2,1)}, bf16[512,2048]{1,0:T(8,128)(2,1)}, bf16[512,2048]{1,0:T(8,128)(2,1)}, bf16[512,2048]{1,0:T(8,128)(2,1)}) custom-call(f32[16,8,4]{2,1,0:T(8,128)} %slice_multiply_fusion.lam, s32[8]{0:T(128)} %compare_convert_fusion.pick, bf16[512,2048]{1,0:T(8,128)(2,1)} %q.1, bf16[512,2048]{1,0:T(8,128)(2,1)} %k.1, ...), custom_call_target="tpu_custom_call" | custom-call | tf_op jit(solution)/shard_map/cross/pallas_call | solution.py:226
  (13 shorter events, 0.1 us)
Async XLA Ops:
  20.2 2.9 %collective-permute-start = (bf16[4,8,128,128]{3,2,1,0:T(8,128)(2,1)S(1)}, bf16[4,8,128,128]{3,2,1,0:T(8,128)(2,1)}, u32[]{:S(2)}, u32[]{:S(2)}) collective-permute-start(bf16[4,8,128,128]{3,2,1,0:T(8,128)(2,1)S(1)} %constant_dynamic-slice_fusion), channel_id=1, source_target_pairs={{0,1},{1,0},{2,3},{3,2},{4,5},{5,4},{6,7},{7,6},{8,9},{9,8},{10,11... | collective-permute-start | bytes 3145736 | tf_op jit(solution)/shard_map/ppermute | solution.py:179
  24.6 2.1 %copy-start.2 = (bf16[4,8,128,128]{3,2,1,0:T(8,128)(2,1)}, bf16[4,8,128,128]{3,2,1,0:T(8,128)(2,1)S(1)}, u32[]{:S(2)}) copy-start(bf16[4,8,128,128]{3,2,1,0:T(8,128)(2,1)S(1)} %add_convert_fusion.after) | copy-start | bytes 3145732
  24.7 25.9 %collective-permute-start.1 = (bf16[4,8,128,128]{3,2,1,0:T(8,128)(2,1)S(1)}, bf16[4,8,128,128]{3,2,1,0:T(8,128)(2,1)}, u32[]{:S(2)}, u32[]{:S(2)}) collective-permute-start(bf16[4,8,128,128]{3,2,1,0:T(8,128)(2,1)S(1)} %add_convert_fusion.after), channel_id=1, source_target_pairs={{0,2},{1,3},{2,0},{3,1},{4,6},{5,7},{6,4},{7,5},{8,10},{9,11},{10,... | collective-permute-start | bytes 3145736 | tf_op jit(solution)/shard_map/ppermute | solution.py:179
  40.0 14.0 %copy-start.3 = (bf16[4,8,128,128]{3,2,1,0:T(8,128)(2,1)S(1)}, bf16[4,8,128,128]{3,2,1,0:T(8,128)(2,1)}, u32[]{:S(2)}) copy-start(bf16[4,8,128,128]{3,2,1,0:T(8,128)(2,1)} %copy-done.2) | copy-start | bytes 3145732
  52.6 1.3 %copy-start = (f32[4,8,128,128]{3,2,1,0:T(8,128)}, f32[4,8,128,128]{3,2,1,0:T(8,128)S(1)}, u32[]{:S(2)}) copy-start(f32[4,8,128,128]{3,2,1,0:T(8,128)S(1)} %convert_add_fusion) | copy-start | bytes 6291460
  54.2 1.9 %copy-start.4 = (bf16[3,8,128,128]{3,2,1,0:T(8,128)(2,1)}, bf16[3,8,128,128]{3,2,1,0:T(8,128)(2,1)S(1)}, u32[]{:S(2)}) copy-start(bf16[3,8,128,128]{3,2,1,0:T(8,128)(2,1)S(1)} %fusion.after) | copy-start | bytes 2359300
  54.2 19.4 %collective-permute-start.3 = (bf16[3,8,128,128]{3,2,1,0:T(8,128)(2,1)S(1)}, bf16[3,8,128,128]{3,2,1,0:T(8,128)(2,1)S(1)}, u32[]{:S(2)}, u32[]{:S(2)}) collective-permute-start(bf16[3,8,128,128]{3,2,1,0:T(8,128)(2,1)S(1)} %fusion.after), channel_id=1, source_target_pairs={{0,4},{4,0},{8,12},{12,8},{1,5},{5,1},{9,13},{13,9},{2,6},{6,2},{1... | collective-permute-start | bytes 2359304 | tf_op jit(solution)/shard_map/ppermute | solution.py:181
  69.3 5.1 %copy-start.5 = (bf16[3,8,128,128]{3,2,1,0:T(8,128)(2,1)S(1)}, bf16[3,8,128,128]{3,2,1,0:T(8,128)(2,1)}, u32[]{:S(2)}) copy-start(bf16[3,8,128,128]{3,2,1,0:T(8,128)(2,1)} %copy-done.4) | copy-start | bytes 2359300
  74.6 13.8 %collective-permute-start.4 = (bf16[8,128,128]{2,1,0:T(8,128)(2,1)S(1)}, bf16[8,128,128]{2,1,0:T(8,128)(2,1)S(1)}, u32[]{:S(2)}, u32[]{:S(2)}) collective-permute-start(bf16[8,128,128]{2,1,0:T(8,128)(2,1)S(1)} %fusion.8), channel_id=1, source_target_pairs={{0,8},{4,12},{8,0},{12,4},{1,9},{5,13},{9,1},{13,5},{2,10},{6,14},... | collective-permute-start | bytes 786440 | tf_op jit(solution)/shard_map/ppermute | solution.py:181
  89.5 2.6 %copy-start.8 = (f32[16,8,21]{2,1,0:T(8,128)S(1)}, f32[16,8,21]{2,1,0:T(8,128)}, u32[]{:S(2)}) copy-start(f32[16,8,21]{2,1,0:T(8,128)} %fusion.9.lam) | copy-start | bytes 32260
  89.7 5.5 %copy-start.1 = (bf16[4,8,128,128]{3,2,1,0:T(8,128)(2,1)}, bf16[4,8,128,128]{3,2,1,0:T(8,128)(2,1)S(1)}, u32[]{:S(2)}) copy-start(bf16[4,8,128,128]{3,2,1,0:T(8,128)(2,1)S(1)} %pad_maximum_fusion.ours) | copy-start | bytes 3145732
  89.7 4.5 %collective-permute-start.5 = (bf16[4,8,128,128]{3,2,1,0:T(8,128)(2,1)S(1)}, bf16[4,8,128,128]{3,2,1,0:T(8,128)(2,1)S(1)}, u32[]{:S(2)}, u32[]{:S(2)}) collective-permute-start(bf16[4,8,128,128]{3,2,1,0:T(8,128)(2,1)S(1)} %pad_maximum_fusion.ours), channel_id=1, source_target_pairs={{0,1},{1,0},{2,3},{3,2},{4,5},{5,4},{6,7},{7,6},{8,9},{9,8},{10,11... | collective-permute-start | bytes 3145736 | tf_op jit(solution)/shard_map/ppermute | solution.py:179
  91.3 2.0 %collective-permute-start.2 = (bf16[16,128,128]{2,1,0:T(8,128)(2,1)S(1)}, bf16[16,128,128]{2,1,0:T(8,128)(2,1)S(1)}, u32[]{:S(2)}, u32[]{:S(2)}) collective-permute-start(bf16[16,128,128]{2,1,0:T(8,128)(2,1)S(1)} %fusion.6), channel_id=1, source_target_pairs={{0,1},{1,0},{2,3},{3,2},{4,5},{5,4},{6,7},{7,6},{8,9},{9,8},{10,11... | collective-permute-start | bytes 1572872 | tf_op jit(solution)/shard_map/ppermute | solution.py:179
  93.3 1.9 %copy-start.6 = (bf16[16,128,128]{2,1,0:T(8,128)(2,1)}, bf16[16,128,128]{2,1,0:T(8,128)(2,1)S(1)}, u32[]{:S(2)}) copy-start(bf16[16,128,128]{2,1,0:T(8,128)(2,1)S(1)} %collective-permute-done.2.x0) | copy-start | bytes 1572868
  94.2 1.0 copy-start.7

commit v3 on v2

--- a/solution.py
+++ b/solution.py
@@ -44,8 +44,8 @@
             out[bits - j, n] = outer[:, j * width : (j + 1) * width].astype(BF16)
 
 
-def dense_kernel(lam, a, b, x, y, after, o1, o2, token, prob):
-    del after
+def dense_kernel(first, lam, a, b, x, y, *refs):
+    o1, o2, token, prob = refs[-4:]
     tok = a.shape[0]
     width = a.shape[1] // GROUP
     token[...] = jnp.zeros_like(token)
@@ -59,7 +59,7 @@
     level = jnp.where(ci <= ri, level, -1)
     big = min(256, tok)
     for n in range(GROUP):
-        head = pl.program_id(0) * GROUP + n
+        head = (pl.program_id(0) + first) * GROUP + n
         lanes = slice(n * width, (n + 1) * width)
         for r0 in range(0, tok, big):
             cols = r0 + big
@@ -91,16 +91,18 @@
 
 
 def cross_kernel(
-    bits, lam, pick, q, k, v, g, o_in, dq_in, dk_in, dv_in, x0, ours, theirs, r0, o, dq, dk, dv
+    bits, lam, pick, q, k, v, g, o_in, dq_in, dk_in, dv_in, x0, ours, theirs, o, dq, dk, dv
 ):
     tok = q.shape[0]
     width = q.shape[1] // GROUP
     own = pick[pl.program_id(0)] == 1
+    lower = pick[pl.num_programs(0)] == 1
     for n in range(GROUP):
         head = pl.program_id(0) * GROUP + n
         lanes = slice(n * width, (n + 1) * width)
         rest = [jnp.where(own, ours[j, n], theirs[j, n]) for j in range(bits)]
-        back = (rest[bits - 1].astype(F32) + r0[n].astype(F32)).astype(BF16)
+        back = rest[bits - 1].astype(F32) + jnp.where(lower, x0[n].astype(F32), 0.0)
+        back = back.astype(BF16)
         dk[:, lanes] = (dk_in[:, lanes].astype(F32) + mm(v[:, lanes], back, NT)).astype(BF16)
         dv[:, lanes] = (dv_in[:, lanes].astype(F32) + mm(k[:, lanes], back, NN)).astype(BF16)
         states = [x0[n]] + rest[: bits - 1]
@@ -158,20 +160,27 @@
         name="states",
     )(lam, queries, keys, values, out_grad)
 
-    def dense(a, b, x, y, after, name):
+    groups = heads // GROUP
+
+    def dense(arrays, first, count, into, after, name):
+        part_spec = pl.BlockSpec((tok, GROUP * width), lambda h: (0, h + first))
+        anywhere = pl.BlockSpec(memory_space=pl.ANY)
         return pl.pallas_call(
-            dense_kernel,
-            grid=(heads // GROUP,),
-            in_specs=[smem] + [row_spec] * 4 + [pl.BlockSpec(memory_space=pl.ANY)],
-            out_specs=[row_spec] * 2 + [pl.BlockSpec((8, 128), lambda h: (0, 0))],
+            functools.partial(dense_kernel, first),
+            grid=(count,),
+            in_specs=[smem] + [part_spec] * 4 + [anywhere] * (len(into) + len(after)),
+            out_specs=[part_spec] * 2 + [pl.BlockSpec((8, 128), lambda h: (0, 0))],
             out_shape=[row_shape] * 2 + [jax.ShapeDtypeStruct((8, 128), F32)],
+            input_output_aliases={5 + i: i for i in range(len(into))},
             scratch_shapes=[pltpu.VMEM((GROUP, tok, tok), BF16)],
             compiler_params=params,
             cost_estimate=pl.CostEstimate(
-                flops=8 * heads * tok * tok * width, bytes_accessed=6 * n_bytes, transcendentals=0
+                flops=8 * count * GROUP * tok * tok * width,
+                bytes_accessed=6 * n_bytes * count // groups,
+                transcendentals=0,
             ),
             name=name,
-        )(lam, a, b, x, y, after)
+        )(lam, *arrays, *into, *after)
 
     def swap(array, bit):
         if bit < head_bits:
@@ -187,53 +196,90 @@
     core = head_i & 1
     got_full = swap(jnp.where(bit_of(0), packet[bits], packet[0]), 0)
     state0 = got_full
-    back0 = jnp.where(bit_of(0), jnp.zeros_like(got_full), got_full)
     keep_i, send_i = core * half, (1 - core) * half
     sent = lax.dynamic_slice_in_dim(packet[:bits], send_i, half, axis=1)
     kept = lax.dynamic_slice_in_dim(packet[:bits], keep_i, half, axis=1)
     run = (kept.astype(F32) + swap(sent, 0).astype(F32)).astype(BF16)
+    forward = (queries, keys, values, out_grad)
+    backward = (out_grad, values, keys, queries)
+    dense_parts = {}
+
+    def dense_out(after):
+        *dense_parts["out"], token = dense(forward, 0, groups, (), after, "dense_out")
+        return token
+
+    def dense_low(after):
+        *dense_parts["grad"], token = dense(backward, 0, groups // 2, (), after, "dense_low")
+        return token
+
+    def dense_high(after):
+        *dense_parts["grad"], token = dense(
+            backward, groups // 2, groups - groups // 2, dense_parts["grad"], after, "dense_high"
+        )
+        return token
+
+    work = [dense_out, dense_low, dense_high]
+
+    def beside(sent, last):
+        zero = 0.0
+        while work:
+            zero = zero + work.pop(0)([sent, state0] if last else [sent])[0, 0]
+            if not last:
+                break
+        return zero
+
+    quarter = half // 2
+    side = head_i >> 1 & 1
+    square = (width, width)
+    whole = jnp.where(bit_of(1), run[-1], run[0])
+    away = lax.dynamic_slice_in_dim(run[:-1], (1 - side) * quarter, quarter, axis=1)
+    stay = lax.dynamic_slice_in_dim(run[:-1], side * quarter, quarter, axis=1)
+    sent = jnp.concatenate([whole.reshape((2, quarter) + square), away], axis=0)
+    got = swap(sent, 1)
+    state1 = got[:2].reshape((half,) + square)
+    run = (stay.astype(F32) + got[2:].astype(F32) + beside(sent, False)).astype(BF16)
     states = []
-    back = jnp.zeros((half, width, width), F32)
-    work = [
-        (queries, keys, values, out_grad, "dense_out"),
-        (out_grad, values, keys, queries, "dense_grad"),
-    ]
-    parts = []
-    for bit in range(1, bits):
+    back = jnp.zeros((quarter,) + square, F32)
+    for bit in range(2, bits):
         last = bit == bits - 1
         sent = jnp.where(bit_of(bit), run[1], run[0]) if last else run
-        got = swap(sent, bit).astype(F32)
-        while work and (len(parts) < bit or last):
-            *arrays, name = work.pop(0)
-            first, second, token = dense(*arrays, sent, name)
-            parts += [(first, second)]
-            got = got + token[0, 0]
+        got = swap(sent, bit)
+        zero = beside(sent, last)
         if last:
-            states.append(got.astype(BF16))
-            back = back + jnp.where(bit_of(bit), 0.0, got)
+            states.append((got.astype(F32) + zero).astype(BF16))
+            back = back + jnp.where(bit_of(bit), 0.0, got.astype(F32))
         else:
-            states.append(got[0].astype(BF16))
-            back = back + jnp.where(bit_of(bit), 0.0, got[-1])
-            run = (run[:-1].astype(F32) + got[:-1]).astype(BF16)
-    (o_part, dv_part), (dq_part, dk_part) = parts
-    ours = jnp.stack(states + [back.astype(BF16)], axis=0)
+            states.append(got[0])
+            back = back + jnp.where(bit_of(bit), 0.0, got[-1].astype(F32))
+            run = (run[:-1].astype(F32) + got[:-1].astype(F32) + zero).astype(BF16)
+    near = jnp.stack(states + [back.astype(BF16)], axis=0)
+    far = swap(near, 1)
+    both = jnp.where(
+        bit_of(1), jnp.concatenate([far, near], axis=1), jnp.concatenate([near, far], axis=1)
+    )
+    back1 = jnp.where(bit_of(1), 0.0, state1.astype(F32))
+    total = (both[-1].astype(F32) + back1).astype(BF16)
+    ours = jnp.concatenate([state1[None], both[:-1], total[None]], axis=0)
     theirs = swap(ours, 0)
+    o_part, dv_part = dense_parts["out"]
+    dq_part, dk_part = dense_parts["grad"]
     steps = half // GROUP
-    pick = (jnp.arange(heads // GROUP, dtype=jnp.int32) // steps == core).astype(jnp.int32)
+    pick = (jnp.arange(groups, dtype=jnp.int32) // steps == core).astype(jnp.int32)
+    pick = jnp.concatenate([pick, (1 - core).astype(jnp.int32)[None]])
 
     mat_spec = pl.BlockSpec((GROUP, width, width), lambda h: (h, 0, 0))
     half_spec = pl.BlockSpec((bits, GROUP, width, width), lambda h: (0, h % steps, 0, 0))
     return pl.pallas_call(
         functools.partial(cross_kernel, bits),
         grid=(heads // GROUP,),
-        in_specs=[smem] * 2 + [row_spec] * 8 + [mat_spec, half_spec, half_spec, mat_spec],
+        in_specs=[smem] * 2 + [row_spec] * 8 + [mat_spec, half_spec, half_spec],
         out_specs=[row_spec] * 4,
         out_shape=[row_shape] * 4,
         compiler_params=params,
         name="cross",
     )(
         lam_cross, pick, queries, keys, values, out_grad,
-        o_part, dq_part, dk_part, dv_part, state0, ours, theirs, back0,
+        o_part, dq_part, dk_part, dv_part, state0, ours, theirs,
     )
 
 

time: 111 us -> 103 us (0.928)
  waiting for transfers between devices: 25.1 us -> 13.3 us
  Pallas kernels: 50 us -> 52.5 us
  starting transfers between devices: 7.29 us -> 8.65 us
    ppermute x2, waiting for transfers between devices: 12.9 us -> 0.01 us  [swap(): return lax.ppermute(array, 'ctx', [(i, i ^ step) for i in range(ctx_n)])]
    add x2 -> x0, other arithmetic: 2.96 us -> none  [shards(): got = got + token[0, 0]]
    pallas_call x2 -> x3, Pallas kernels: 26.5 us -> 29.1 us  [dense(): pl.pallas_call(functools.partial(dense_kernel, first), grid=(count,), in_...]
    convert_element_type x3 -> x4, other arithmetic: 0.85 us -> 3.48 us  [the longest x1 1.78 us: shards(): (stay.astype(F32) + got[2:].astype(F32) + beside(sent, False)).astype(BF16)]
    ppermute x4 -> x5, starting transfers between devices: 2.82 us -> 4.11 us  [swap(): return lax.ppermute(array, 'head', pairs)]
    ppermute x4 -> x5, waiting for transfers between devices: 12.2 us -> 13.3 us  [swap(): return lax.ppermute(array, 'head', pairs)]
    slice x4 -> x7, local copies, waits for them, and re-layouts: 3.74 us -> 4.67 us  [the longest x3 3.6 us: beside(): zero = zero + work.pop(0)([sent, state0] if last else [sent])[0, 0]]
    unnamed x19 -> x15, local copies, waits for them, and re-layouts: 3.05 us -> 2.51 us
  transfers between devices with their start and end apart: 6 -> 7, of which waited for: 5 -> 4; matrix products, arithmetic and copies ran while one was open for 7% -> 10% of each run, Pallas kernels for 24% -> 29%
where the time goes in v3:
time: 103 us; the launch traced here: 102 us
  Pallas kernels  52.5 us (51%)
  waiting for transfers between devices  13.3 us (13%)
  other arithmetic  10.6 us (10%)
  local copies, waits for them, and re-layouts  9.8 us (10%)
  starting transfers between devices  8.65 us (8%)
  blocking collectives  6.15 us (6%)
    pallas_call x3, Pallas kernels, dense(): pl.pallas_call(functools.partial(dense_kernel, first), grid=(count,), in_...  29.1 us
    pallas_call x1, Pallas kernels, shards(): pl.pallas_call(functools.partial(cross_kernel, bits), grid=(heads // GROU...  14.2 us
    ppermute x5, waiting for transfers between devices, swap(): return lax.ppermute(array, 'head', pairs)  13.3 us
    pallas_call x1, Pallas kernels, shards(): pl.pallas_call(functools.partial(state_kernel, bits, low), grid=(heads //...  9.12 us
    all_gather x1, blocking collectives, shards(): table = lax.all_gather(level_table, 'head', axis=2, tiled=True)  6.15 us
    ppermute x2, starting transfers between devices, swap(): return lax.ppermute(array, 'ctx', [(i, i ^ step) for i in range(ctx_n)])  4.54 us
    ppermute x5, starting transfers between devices, swap(): return lax.ppermute(array, 'head', pairs)  4.11 us
    slice x3, local copies, waits for them, and re-layouts, beside(): zero = zero + work.pop(0)([sent, state0] if last else [sent])[0, 0]  3.6 us
  transfers between devices with their start and end apart: 7, of which 4 were waited for; matrix products, arithmetic and copies ran while one was open for 10% of the time, Pallas kernels for 29%

profile of v3, /device:TPU:0, one launch (start us, length us, event | category | flops | bytes accessed | tf_op | source)
XLA Modules:
  0.0 101.8 jit_solution(4765176736996554908)
XLA Ops:
  0.7 0.7 dynamic_slice.15
  1.4 0.1 fusion.8
  1.5 0.7 copy.15
  2.2 6.1 %all_gather.3 = f32[8,21,16]{1,0,2:T(8,128)S(1)} all-gather(f32[8,21,4]{1,0,2:T(8,128)S(1)} %copy.15), channel_id=1, replica_groups=mesh['grp'=2,'ctx'=4,'head'=4] {'head'}, dimensions={2}, use_global_device_ids=true | all-gather | bytes 13440 | tf_op jit(solution)/shard_map/all_gather | solution.py:135
  8.3 0.1 multiply_reduce_fusion
  8.5 0.7 fusion.7.lam
  9.1 9.1 %states.1 = bf16[5,16,128,128]{3,2,1,0:T(8,128)(2,1)} custom-call(f32[16,8,21]{2,1,0:T(8,128)} %fusion.7.lam, bf16[512,2048]{1,0:T(8,128)(2,1)} %q.1, bf16[512,2048]{1,0:T(8,128)(2,1)} %k.1, bf16[512,2048]{1,0:T(8,128)(2,1)} %v.1, bf16[512,2048]{1,0:T(8,128)(2,1)} %g.1), custom_call_target="tpu_custom_call" | custom-call | tf_op jit(solution)/shard_map/states/pallas_call | solution.py:153
  18.3 1.7 %slice.83 = bf16[4,16,128,128]{3,2,1,0:T(8,128)(2,1)S(1)} slice(bf16[5,16,128,128]{3,2,1,0:T(8,128)(2,1)} %states.1), slice={[0:4], [0:16], [0:128], [0:128]} | slice | bytes 4194304 | tf_op jit(solution)/shard_map/slice | solution.py:201
  20.0 0.1 constant_dynamic-slice_fusion.1
  20.1 0.4 collective-permute-start
  20.5 2.5 %collective-permute-done = bf16[4,8,128,128]{3,2,1,0:T(8,128)(2,1)} collective-permute-done((bf16[4,8,128,128]{3,2,1,0:T(8,128)(2,1)S(1)}, bf16[4,8,128,128]{3,2,1,0:T(8,128)(2,1)}, u32[]{:S(2)}, u32[]{:S(2)}) %collective-permute-start) | collective-permute-done | bytes 1048608 | tf_op jit(solution)/shard_map/ppermute | solution.py:188
  23.0 1.6 %add_convert_fusion = bf16[4,8,128,128]{3,2,1,0:T(8,128)(2,1)S(1)} fusion(bf16[4,8,128,128]{3,2,1,0:T(8,128)(2,1)} %collective-permute-done, bf16[4,16,128,128]{3,2,1,0:T(8,128)(2,1)S(1)} %slice.83, s32[]{:T(128)S(6)} %select_n.94), kind=kLoop, calls=%fused_computation | loop fusion | flops 2097152 | bytes 3145732 | tf_op jit(solution)/shard_map/convert_element_type | solution.py:202
  24.6 0.1 slice.86
  24.7 0.1 pad_maximum_fusion.1.refs_0_
  24.8 0.0 copy-start.5
  24.8 2.1 %collective-permute-start.1 = (bf16[5,4,128,128]{3,2,1,0:T(8,128)(2,1)S(1)}, bf16[5,4,128,128]{3,2,1,0:T(8,128)(2,1)}, u32[]{:S(2)}, u32[]{:S(2)}) collective-permute-start(bf16[5,4,128,128]{3,2,1,0:T(8,128)(2,1)S(1)} %pad_maximum_fusion.1.refs_0_), channel_id=1, source_target_pairs={{0,2},{1,3},{2,0},{3,1},{4,6},{5,7},{6,4},{7,5},{8,10},{9,11},{10,... | collective-permute-start | bytes 1966088 | tf_op jit(solution)/shard_map/ppermute | solution.py:188
  26.9 13.3 %dense_out.1 = (bf16[512,2048]{1,0:T(8,128)(2,1)}, bf16[512,2048]{1,0:T(8,128)(2,1)}, f32[8,128]{1,0:T(8,128)}) custom-call(f32[16,8,21]{2,1,0:T(8,128)} %fusion.7.lam, bf16[512,2048]{1,0:T(8,128)(2,1)} %q.1, bf16[512,2048]{1,0:T(8,128)(2,1)} %k.1, bf16[512,2048]{1,0:T(8,128)(2,1)} %v.1, bf16[512,2048]{1,0:T(8,128)(2,1)} %g.1, bf16[5,4,128,128]{3,2,1,0:T(8,128)(2,1)} %copy-done.5), custom_call_target="tpu_custom_call" | custom-call | flops 4294967296 | bytes 12582912 | tf_op jit(solution)/shard_map/dense_out/pallas_call | solution.py:168
  40.1 1.2 %slice.68 = f32[1,1]{1,0:T(1,128)} slice(f32[8,128]{1,0:T(8,128)} %get-tuple-element.14), slice={[0:1], [0:1]} | slice | bytes 8 | tf_op jit(solution)/shard_map/slice | solution.py:226
  41.3 0.9 collective-permute-done.1
  42.2 1.8 %add_convert_fusion.1.refs_0_ = bf16[3,4,128,128]{3,2,1,0:T(8,128)(2,1)S(1)} fusion(bf16[5,4,128,128]{3,2,1,0:T(8,128)(2,1)} %collective-permute-done.1, f32[]{:T(128)} %bitcast.3, bf16[3,8,128,128]{3,2,1,0:T(8,128)(2,1)S(1)} %slice.86, s32[]{:T(128)S(6)} %select_n.99), kind=kLoop, calls=%fused_computation.3 | loop fusion | flops 983040 | bytes 1179656 | tf_op jit(solution)/shard_map/convert_element_type | solution.py:240
  44.0 0.0 copy-start.1
  44.0 1.9 %collective-permute-start.2 = (bf16[3,4,128,128]{3,2,1,0:T(8,128)(2,1)S(1)}, bf16[3,4,128,128]{3,2,1,0:T(8,128)(2,1)S(1)}, u32[]{:S(2)}, u32[]{:S(2)}) collective-permute-start(bf16[3,4,128,128]{3,2,1,0:T(8,128)(2,1)S(1)} %add_convert_fusion.1.refs_0_), channel_id=1, source_target_pairs={{0,4},{4,0},{8,12},{12,8},{1,5},{5,1},{9,13},{13,9},{2,6},{6,2},{1... | collective-permute-start | bytes 1179656 | tf_op jit(solution)/shard_map/ppermute | solution.py:190
  45.9 2.0 %fusion = bf16[16,128,128]{2,1,0:T(8,128)(2,1)} fusion(bf16[5,16,128,128]{3,2,1,0:T(8,128)(2,1)} %states.1, pred[]{:T(512)S(6)} %eq.45), kind=kLoop, calls=%fused_computation.6 | loop fusion | flops 262144 | bytes 1572865 | tf_op jit(solution)/shard_map/jit(_where)/select_n | solution.py:197
  47.9 0.0 collective-permute-start.3
  47.9 8.0 %dense_low.1 = (bf16[512,2048]{1,0:T(8,128)(2,1)}, bf16[512,2048]{1,0:T(8,128)(2,1)}, f32[8,128]{1,0:T(8,128)}) custom-call(f32[16,8,21]{2,1,0:T(8,128)} %fusion.7.lam, bf16[512,2048]{1,0:T(8,128)(2,1)} %g.1, bf16[512,2048]{1,0:T(8,128)(2,1)} %v.1, bf16[512,2048]{1,0:T(8,128)(2,1)} %k.1, bf16[512,2048]{1,0:T(8,128)(2,1)} %q.1, bf16[3,4,128,128]{3,2,1,0:T(8,128)(2,1)} %copy-done.1), custom_call_target="tpu_custom_call" | custom-call | flops 2147483648 | bytes 6291456 | tf_op jit(solution)/shard_map/dense_low/pallas_call | solution.py:168
  55.9 1.2 %slice.71 = f32[1,1]{1,0:T(1,128)} slice(f32[8,128]{1,0:T(8,128)} %get-tuple-element.17), slice={[0:1], [0:1]} | slice | bytes 8 | tf_op jit(solution)/shard_map/slice | solution.py:226
  57.1 1.6 %add_convert_fusion.3 = bf16[2,4,128,128]{3,2,1,0:T(8,128)(2,1)S(1)} fusion(bf16[3,4,128,128]{3,2,1,0:T(8,128)(2,1)S(1)} %collective-permute-done.2, bf16[3,4,128,128]{3,2,1,0:T(8,128)(2,1)} %copy-done.1, f32[]{:T(128)} %bitcast.4), kind=kLoop, calls=%fused_computation.8 | loop fusion | flops 655360 | bytes 786436 | tf_op jit(solution)/shard_map/convert_element_type | solution.py:254
  58.8 0.0 copy-start.6
  58.8 2.7 %collective-permute-start.4 = (bf16[4,128,128]{2,1,0:T(8,128)(2,1)S(1)}, bf16[4,128,128]{2,1,0:T(8,128)(2,1)S(1)}, u32[]{:S(2)}, u32[]{:S(2)}) collective-permute-start(bf16[4,128,128]{2,1,0:T(8,128)(2,1)S(1)} %fusion.6.refs_2_), channel_id=1, source_target_pairs={{0,8},{4,12},{8,0},{12,4},{1,9},{5,13},{9,1},{13,5},{2,10},{6,14},... | collective-permute-start | bytes 393224 | tf_op jit(solution)/shard_map/ppermute | solution.py:190
  61.4 0.0 collective-permute-done.3.refs_3_.x0
  61.4 0.8 copy-done.2
  62.2 7.9 %dense_high.1 = (bf16[512,2048]{1,0:T(8,128)(2,1)}, bf16[512,2048]{1,0:T(8,128)(2,1)}, f32[8,128]{1,0:T(8,128)}) custom-call(f32[16,8,21]{2,1,0:T(8,128)} %fusion.7.lam, bf16[512,2048]{1,0:T(8,128)(2,1)} %g.1, bf16[512,2048]{1,0:T(8,128)(2,1)} %v.1, bf16[512,2048]{1,0:T(8,128)(2,1)} %k.1, ...), custom_call_target="tpu_custom_call", output_to_operand_aliasing={{0}: (5, {}), {1}: (6, {})} | custom-call | flops 2147483648 | bytes 6291456 | tf_op jit(solution)/shard_map/dense_high/pallas_call | solution.py:168
  70.2 1.2 %slice.78 = f32[1,1]{1,0:T(1,128)} slice(f32[8,128]{1,0:T(8,128)} %get-tuple-element.21), slice={[0:1], [0:1]} | slice | bytes 8 | tf_op jit(solution)/shard_map/slice | solution.py:226
  71.4 0.0 collective-permute-done.4
  71.4 0.7 fusion.5
  72.2 1.6 %collective-permute-start.5 = (bf16[3,4,128,128]{3,2,1,0:T(8,128)(2,1)S(1)}, bf16[3,4,128,128]{3,2,1,0:T(8,128)(2,1)S(1)}, u32[]{:S(2)}, u32[]{:S(2)}) collective-permute-start(bf16[3,4,128,128]{3,2,1,0:T(8,128)(2,1)S(1)} %pad_maximum_fusion.2), channel_id=1, source_target_pairs={{0,2},{1,3},{2,0},{3,1},{4,6},{5,7},{6,4},{7,5},{8,10},{9,11},{10,... | collective-permute-start | bytes 1179656 | tf_op jit(solution)/shard_map/ppermute | solution.py:188
  73.7 1.0 slice.94
  74.7 8.8 %collective-permute-done.5 = bf16[3,4,128,128]{3,2,1,0:T(8,128)(2,1)S(1)} collective-permute-done((bf16[3,4,128,128]{3,2,1,0:T(8,128)(2,1)S(1)}, bf16[3,4,128,128]{3,2,1,0:T(8,128)(2,1)S(1)}, u32[]{:S(2)}, u32[]{:S(2)}) %collective-permute-start.5) | collective-permute-done | bytes 393248 | tf_op jit(solution)/shard_map/ppermute | solution.py:188
  83.5 0.1 maximum_select_fusion
  83.6 0.0 copy-start.3
  83.6 0.1 add_convert_fusion.2
  83.7 0.1 pad_maximum_fusion.ours
  83.9 0.1 collective-permute-start.6
  84.0 0.8 pad_add_fusion.pick
  84.8 0.7 slice_multiply_fusion.lam
  85.5 1.1 %collective-permute-done.6.theirs = bf16[4,8,128,128]{3,2,1,0:T(8,128)(2,1)S(1)} collective-permute-done((bf16[4,8,128,128]{3,2,1,0:T(8,128)(2,1)S(1)}, bf16[4,8,128,128]{3,2,1,0:T(8,128)(2,1)S(1)}, u32[]{:S(2)}, u32[]{:S(2)}) %collective-permute-start.6) | collective-permute-done | bytes 1048608 | tf_op jit(solution)/shard_map/ppermute | solution.py:188
  86.6 1.0 copy-done.4
  87.6 14.2 %cross.1 = (bf16[512,2048]{1,0:T(8,128)(2,1)}, bf16[512,2048]{1,0:T(8,128)(2,1)}, bf16[512,2048]{1,0:T(8,128)(2,1)}, bf16[512,2048]{1,0:T(8,128)(2,1)}) custom-call(f32[16,8,4]{2,1,0:T(8,128)} %slice_multiply_fusion.lam, s32[9]{0:T(128)} %pad_add_fusion.pick, bf16[512,2048]{1,0:T(8,128)(2,1)} %q.1, bf16[512,2048]{1,0:T(8,128)(2,1)} %k.1, ...), custom_call_target="tpu_custom_call" | custom-call | tf_op jit(solution)/shard_map/cross/pallas_call | solution.py:272
  (19 shorter events, 0.2 us)
Async XLA Ops:
  20.1 2.9 %collective-permute-start = (bf16[4,8,128,128]{3,2,1,0:T(8,128)(2,1)S(1)}, bf16[4,8,128,128]{3,2,1,0:T(8,128)(2,1)}, u32[]{:S(2)}, u32[]{:S(2)}) collective-permute-start(bf16[4,8,128,128]{3,2,1,0:T(8,128)(2,1)S(1)} %constant_dynamic-slice_fusion.1), channel_id=1, source_target_pairs={{0,1},{1,0},{2,3},{3,2},{4,5},{5,4},{6,7},{7,6},{8,9},{9,8},{10,11... | collective-permute-start | bytes 3145736 | tf_op jit(solution)/shard_map/ppermute | solution.py:188
  24.8 2.1 %copy-start.5 = (bf16[5,4,128,128]{3,2,1,0:T(8,128)(2,1)}, bf16[5,4,128,128]{3,2,1,0:T(8,128)(2,1)S(1)}, u32[]{:S(2)}) copy-start(bf16[5,4,128,128]{3,2,1,0:T(8,128)(2,1)S(1)} %pad_maximum_fusion.1.refs_0_) | copy-start | bytes 1966084
  24.8 17.4 %collective-permute-start.1 = (bf16[5,4,128,128]{3,2,1,0:T(8,128)(2,1)S(1)}, bf16[5,4,128,128]{3,2,1,0:T(8,128)(2,1)}, u32[]{:S(2)}, u32[]{:S(2)}) collective-permute-start(bf16[5,4,128,128]{3,2,1,0:T(8,128)(2,1)S(1)} %pad_maximum_fusion.1.refs_0_), channel_id=1, source_target_pairs={{0,2},{1,3},{2,0},{3,1},{4,6},{5,7},{6,4},{7,5},{8,10},{9,11},{10,... | collective-permute-start | bytes 1966088 | tf_op jit(solution)/shard_map/ppermute | solution.py:188
  44.0 4.0 %copy-start.1 = (bf16[3,4,128,128]{3,2,1,0:T(8,128)(2,1)}, bf16[3,4,128,128]{3,2,1,0:T(8,128)(2,1)S(1)}, u32[]{:S(2)}) copy-start(bf16[3,4,128,128]{3,2,1,0:T(8,128)(2,1)S(1)} %add_convert_fusion.1.refs_0_) | copy-start | bytes 1179652
  44.0 13.1 %collective-permute-start.2 = (bf16[3,4,128,128]{3,2,1,0:T(8,128)(2,1)S(1)}, bf16[3,4,128,128]{3,2,1,0:T(8,128)(2,1)S(1)}, u32[]{:S(2)}, u32[]{:S(2)}) collective-permute-start(bf16[3,4,128,128]{3,2,1,0:T(8,128)(2,1)S(1)} %add_convert_fusion.1.refs_0_), channel_id=1, source_target_pairs={{0,4},{4,0},{8,12},{12,8},{1,5},{5,1},{9,13},{13,9},{2,6},{6,2},{1... | collective-permute-start | bytes 1179656 | tf_op jit(solution)/shard_map/ppermute | solution.py:190
  47.9 13.5 %collective-permute-start.3 = (bf16[16,128,128]{2,1,0:T(8,128)(2,1)}, bf16[16,128,128]{2,1,0:T(8,128)(2,1)S(1)}, u32[]{:S(2)}, u32[]{:S(2)}) collective-permute-start(bf16[16,128,128]{2,1,0:T(8,128)(2,1)} %fusion), channel_id=1, source_target_pairs={{0,1},{1,0},{2,3},{3,2},{4,5},{5,4},{6,7},{7,6},{8,9},{9,8},{10,11... | collective-permute-start | bytes 1572872 | tf_op jit(solution)/shard_map/ppermute | solution.py:188
  58.8 2.7 %copy-start.6 = (bf16[4,128,128]{2,1,0:T(8,128)(2,1)}, bf16[4,128,128]{2,1,0:T(8,128)(2,1)S(1)}, u32[]{:S(2)}) copy-start(bf16[4,128,128]{2,1,0:T(8,128)(2,1)S(1)} %fusion.6.refs_2_) | copy-start | bytes 393220
  58.8 12.6 %collective-permute-start.4 = (bf16[4,128,128]{2,1,0:T(8,128)(2,1)S(1)}, bf16[4,128,128]{2,1,0:T(8,128)(2,1)S(1)}, u32[]{:S(2)}, u32[]{:S(2)}) collective-permute-start(bf16[4,128,128]{2,1,0:T(8,128)(2,1)S(1)} %fusion.6.refs_2_), channel_id=1, source_target_pairs={{0,8},{4,12},{8,0},{12,4},{1,9},{5,13},{9,1},{13,5},{2,10},{6,14},... | collective-permute-start | bytes 393224 | tf_op jit(solution)/shard_map/ppermute | solution.py:190
  61.4 0.8 copy-start.2
  72.2 11.3 %collective-permute-start.5 = (bf16[3,4,128,128]{3,2,1,0:T(8,128)(2,1)S(1)}, bf16[3,4,128,128]{3,2,1,0:T(8,128)(2,1)S(1)}, u32[]{:S(2)}, u32[]{:S(2)}) collective-permute-start(bf16[3,4,128,128]{3,2,1,0:T(8,128)(2,1)S(1)} %pad_maximum_fusion.2), channel_id=1, source_target_pairs={{0,2},{1,3},{2,0},{3,1},{4,6},{5,7},{6,4},{7,5},{8,10},{9,11},{10,... | collective-permute-start | bytes 1179656 | tf_op jit(solution)/shard_map/ppermute | solution.py:188
  83.6 1.2 %copy-start.3 = (f32[16,8,21]{2,1,0:T(8,128)S(1)}, f32[16,8,21]{2,1,0:T(8,128)}, u32[]{:S(2)}) copy-start(f32[16,8,21]{2,1,0:T(8,128)} %fusion.7.lam) | copy-start | bytes 32260
  83.9 3.7 %copy-start = (bf16[4,8,128,128]{3,2,1,0:T(8,128)(2,1)}, bf16[4,8,128,128]{3,2,1,0:T(8,128)(2,1)S(1)}, u32[]{:S(2)}) copy-start(bf16[4,8,128,128]{3,2,1,0:T(8,128)(2,1)S(1)} %pad_maximum_fusion.ours) | copy-start | bytes 3145732
  83.9 2.7 %collective-permute-start.6 = (bf16[4,8,128,128]{3,2,1,0:T(8,128)(2,1)S(1)}, bf16[4,8,128,128]{3,2,1,0:T(8,128)(2,1)S(1)}, u32[]{:S(2)}, u32[]{:S(2)}) collective-permute-start(bf16[4,8,128,128]{3,2,1,0:T(8,128)(2,1)S(1)} %pad_maximum_fusion.ours), channel_id=1, source_target_pairs={{0,1},{1,0},{2,3},{3,2},{4,5},{5,4},{6,7},{7,6},{8,9},{9,8},{10,11... | collective-permute-start | bytes 3145736 | tf_op jit(solution)/shard_map/ppermute | solution.py:188
  86.6 1.0 copy-start.4

commit v4 on v3

--- a/solution.py
+++ b/solution.py
@@ -106,18 +106,18 @@
         dk[:, lanes] = (dk_in[:, lanes].astype(F32) + mm(v[:, lanes], back, NT)).astype(BF16)
         dv[:, lanes] = (dv_in[:, lanes].astype(F32) + mm(k[:, lanes], back, NN)).astype(BF16)
         states = [x0[n]] + rest[: bits - 1]
-        fwd = mm(q[:, lanes], jnp.concatenate(states, axis=1), NN)
-        bwd = mm(g[:, lanes], jnp.concatenate(states, axis=0), NT)
-        for c in range(tok // STRETCH):
-            rows = slice(c * STRETCH, (c + 1) * STRETCH)
-            o_sum = o_in[rows, lanes].astype(F32)
-            q_sum = dq_in[rows, lanes].astype(F32)
+        sides = ((q, states, 0, NN, o_in, o), (g, states, 1, NT, dq_in, dq))
+        for rows_in, mats, axis, dims, part, result in sides:
+            full = rows_in[:, lanes].astype(F32)
+            scaled = []
             for j in range(bits):
-                scale = lam[head, c, j]
-                o_sum = o_sum + fwd[rows, j * width : (j + 1) * width] * scale
-                q_sum = q_sum + bwd[rows, j * width : (j + 1) * width] * scale
-            o[rows, lanes] = o_sum.astype(BF16)
-            dq[rows, lanes] = q_sum.astype(BF16)
+                pieces = [
+                    full[c * STRETCH : (c + 1) * STRETCH] * lam[head, c, j]
+                    for c in range(tok // STRETCH)
+                ]
+                scaled.append(jnp.concatenate(pieces, axis=0).astype(BF16))
+            total = mm(jnp.concatenate(scaled, axis=1), jnp.concatenate(mats, axis=axis), dims)
+            result[:, lanes] = (part[:, lanes].astype(F32) + total).astype(BF16)
 
 
 def shards(queries, keys, values, out_grad, level_table, selector):
@@ -220,13 +220,8 @@
 
     work = [dense_out, dense_low, dense_high]
 
-    def beside(sent, last):
-        zero = 0.0
-        while work:
-            zero = zero + work.pop(0)([sent, state0] if last else [sent])[0, 0]
-            if not last:
-                break
-        return zero
+    def beside(sent):
+        return work.pop(0)(sent)[0, 0]
 
     quarter = half // 2
     side = head_i >> 1 & 1
@@ -237,14 +232,14 @@
     sent = jnp.concatenate([whole.reshape((2, quarter) + square), away], axis=0)
     got = swap(sent, 1)
     state1 = got[:2].reshape((half,) + square)
-    run = (stay.astype(F32) + got[2:].astype(F32) + beside(sent, False)).astype(BF16)
+    run = (stay.astype(F32) + got[2:].astype(F32) + beside([sent])).astype(BF16)
     states = []
     back = jnp.zeros((quarter,) + square, F32)
     for bit in range(2, bits):
         last = bit == bits - 1
         sent = jnp.where(bit_of(bit), run[1], run[0]) if last else run
         got = swap(sent, bit)
-        zero = beside(sent, last)
+        zero = beside([sent]) if bit == 2 else 0.0
         if last:
             states.append((got.astype(F32) + zero).astype(BF16))
             back = back + jnp.where(bit_of(bit), 0.0, got.astype(F32))
@@ -253,7 +248,7 @@
             back = back + jnp.where(bit_of(bit), 0.0, got[-1].astype(F32))
             run = (run[:-1].astype(F32) + got[:-1].astype(F32) + zero).astype(BF16)
     near = jnp.stack(states + [back.astype(BF16)], axis=0)
-    far = swap(near, 1)
+    far = (swap(near, 1).astype(F32) + beside([near, state0])).astype(BF16)
     both = jnp.where(
         bit_of(1), jnp.concatenate([far, near], axis=1), jnp.concatenate([near, far], axis=1)
     )

time: 103 us -> 99 us (0.961)
  waiting for transfers between devices: 13.3 us -> 8.98 us
    ppermute x5, waiting for transfers between devices: 13.3 us -> 4.55 us  [swap(): return lax.ppermute(array, 'head', pairs)]
    ppermute x2, waiting for transfers between devices: 0.01 us -> 4.43 us  [swap(): return lax.ppermute(array, 'ctx', [(i, i ^ step) for i in range(ctx_n)])]
    convert_element_type x1 -> x2, other arithmetic: 1.78 us -> 3.5 us  [the longest x1 1.78 us: shards(): run = (stay.astype(F32) + got[2:].astype(F32) + beside([sent])).astype(BF16)]
  transfers between devices with their start and end apart: 7 -> 7, of which waited for: 4 -> 4; matrix products, arithmetic and copies ran while one was open for 10% -> 8% of each run, Pallas kernels for 29% -> 30%
where the time goes in v4:
time: 99 us; the launch traced here: 97.9 us
  Pallas kernels  52.5 us (53%)
  other arithmetic  10.8 us (11%)
  local copies, waits for them, and re-layouts  9.79 us (10%)
  waiting for transfers between devices  8.98 us (9%)
  starting transfers between devices  8.72 us (9%)
  blocking collectives  6.15 us (6%)
    pallas_call x3, Pallas kernels, dense(): pl.pallas_call(functools.partial(dense_kernel, first), grid=(count,), in_...  29.1 us
    pallas_call x1, Pallas kernels, shards(): pl.pallas_call(functools.partial(cross_kernel, bits), grid=(heads // GROU...  14.2 us
    pallas_call x1, Pallas kernels, shards(): pl.pallas_call(functools.partial(state_kernel, bits, low), grid=(heads //...  9.21 us
    all_gather x1, blocking collectives, shards(): table = lax.all_gather(level_table, 'head', axis=2, tiled=True)  6.15 us
    ppermute x5, waiting for transfers between devices, swap(): return lax.ppermute(array, 'head', pairs)  4.55 us
    ppermute x2, starting transfers between devices, swap(): return lax.ppermute(array, 'ctx', [(i, i ^ step) for i in range(ctx_n)])  4.54 us
    ppermute x2, waiting for transfers between devices, swap(): return lax.ppermute(array, 'ctx', [(i, i ^ step) for i in range(ctx_n)])  4.43 us
    ppermute x5, starting transfers between devices, swap(): return lax.ppermute(array, 'head', pairs)  4.18 us
  transfers between devices with their start and end apart: 7, of which 4 were waited for; matrix products, arithmetic and copies ran while one was open for 8% of the time, Pallas kernels for 30%

profile of v4, /device:TPU:0, one launch (start us, length us, event | category | flops | bytes accessed | tf_op | source)
XLA Modules:
  0.0 97.9 jit_solution(7605847798251914983)
XLA Ops:
  0.7 0.7 dynamic_slice.15
  1.4 0.1 fusion.5
  1.5 0.7 copy.15
  2.2 6.1 %all_gather.3 = f32[8,21,16]{1,0,2:T(8,128)S(1)} all-gather(f32[8,21,4]{1,0,2:T(8,128)S(1)} %copy.15), channel_id=1, replica_groups=mesh['grp'=2,'ctx'=4,'head'=4] {'head'}, dimensions={2}, use_global_device_ids=true | all-gather | bytes 13440 | tf_op jit(solution)/shard_map/all_gather | solution.py:135
  8.3 0.1 multiply_reduce_fusion
  8.5 0.7 fusion.4.lam
  9.1 9.2 %states.1 = bf16[5,16,128,128]{3,2,1,0:T(8,128)(2,1)} custom-call(f32[16,8,21]{2,1,0:T(8,128)} %fusion.4.lam, bf16[512,2048]{1,0:T(8,128)(2,1)} %q.1, bf16[512,2048]{1,0:T(8,128)(2,1)} %k.1, bf16[512,2048]{1,0:T(8,128)(2,1)} %v.1, bf16[512,2048]{1,0:T(8,128)(2,1)} %g.1), custom_call_target="tpu_custom_call" | custom-call | tf_op jit(solution)/shard_map/states/pallas_call | solution.py:153
  18.3 1.7 %slice.83 = bf16[4,16,128,128]{3,2,1,0:T(8,128)(2,1)S(1)} slice(bf16[5,16,128,128]{3,2,1,0:T(8,128)(2,1)} %states.1), slice={[0:4], [0:16], [0:128], [0:128]} | slice | bytes 4194304 | tf_op jit(solution)/shard_map/slice | solution.py:201
  20.1 0.1 constant_dynamic-slice_fusion.1
  20.2 0.4 collective-permute-start
  20.6 2.5 %collective-permute-done = bf16[4,8,128,128]{3,2,1,0:T(8,128)(2,1)} collective-permute-done((bf16[4,8,128,128]{3,2,1,0:T(8,128)(2,1)S(1)}, bf16[4,8,128,128]{3,2,1,0:T(8,128)(2,1)}, u32[]{:S(2)}, u32[]{:S(2)}) %collective-permute-start) | collective-permute-done | bytes 1048608 | tf_op jit(solution)/shard_map/ppermute | solution.py:188
  23.1 1.6 %add_convert_fusion = bf16[4,8,128,128]{3,2,1,0:T(8,128)(2,1)S(1)} fusion(bf16[4,8,128,128]{3,2,1,0:T(8,128)(2,1)} %collective-permute-done, bf16[4,16,128,128]{3,2,1,0:T(8,128)(2,1)S(1)} %slice.83, s32[]{:T(128)S(6)} %select_n.95), kind=kLoop, calls=%fused_computation | loop fusion | flops 2097152 | bytes 3145732 | tf_op jit(solution)/shard_map/convert_element_type | solution.py:202
  24.6 0.1 slice.86
  24.8 0.1 pad_maximum_fusion.1.refs_0_
  24.9 0.0 copy-start.6
  24.9 2.1 %collective-permute-start.1 = (bf16[5,4,128,128]{3,2,1,0:T(8,128)(2,1)S(1)}, bf16[5,4,128,128]{3,2,1,0:T(8,128)(2,1)}, u32[]{:S(2)}, u32[]{:S(2)}) collective-permute-start(bf16[5,4,128,128]{3,2,1,0:T(8,128)(2,1)S(1)} %pad_maximum_fusion.1.refs_0_), channel_id=1, source_target_pairs={{0,2},{1,3},{2,0},{3,1},{4,6},{5,7},{6,4},{7,5},{8,10},{9,11},{10,... | collective-permute-start | bytes 1966088 | tf_op jit(solution)/shard_map/ppermute | solution.py:188
  27.0 13.2 %dense_out.1 = (bf16[512,2048]{1,0:T(8,128)(2,1)}, bf16[512,2048]{1,0:T(8,128)(2,1)}, f32[8,128]{1,0:T(8,128)}) custom-call(f32[16,8,21]{2,1,0:T(8,128)} %fusion.4.lam, bf16[512,2048]{1,0:T(8,128)(2,1)} %q.1, bf16[512,2048]{1,0:T(8,128)(2,1)} %k.1, bf16[512,2048]{1,0:T(8,128)(2,1)} %v.1, bf16[512,2048]{1,0:T(8,128)(2,1)} %g.1, bf16[5,4,128,128]{3,2,1,0:T(8,128)(2,1)} %copy-done.6), custom_call_target="tpu_custom_call" | custom-call | flops 4294967296 | bytes 12582912 | tf_op jit(solution)/shard_map/dense_out/pallas_call | solution.py:168
  40.2 1.2 %slice.68 = f32[1,1]{1,0:T(1,128)} slice(f32[8,128]{1,0:T(8,128)} %get-tuple-element.14), slice={[0:1], [0:1]} | slice | bytes 8 | tf_op jit(solution)/shard_map/slice | solution.py:224
  41.4 0.9 collective-permute-done.1
  42.3 1.8 %add_convert_fusion.2.refs_0_ = bf16[3,4,128,128]{3,2,1,0:T(8,128)(2,1)S(1)} fusion(bf16[5,4,128,128]{3,2,1,0:T(8,128)(2,1)} %collective-permute-done.1, f32[]{:T(128)} %bitcast.3, bf16[3,8,128,128]{3,2,1,0:T(8,128)(2,1)S(1)} %slice.86, s32[]{:T(128)S(6)} %select_n.100), kind=kLoop, calls=%fused_computation.4 | loop fusion | flops 983040 | bytes 1179656 | tf_op jit(solution)/shard_map/convert_element_type | solution.py:235
  44.1 0.0 copy-start.1
  44.1 1.9 %collective-permute-start.2 = (bf16[3,4,128,128]{3,2,1,0:T(8,128)(2,1)S(1)}, bf16[3,4,128,128]{3,2,1,0:T(8,128)(2,1)S(1)}, u32[]{:S(2)}, u32[]{:S(2)}) collective-permute-start(bf16[3,4,128,128]{3,2,1,0:T(8,128)(2,1)S(1)} %add_convert_fusion.2.refs_0_), channel_id=1, source_target_pairs={{0,4},{4,0},{8,12},{12,8},{1,5},{5,1},{9,13},{13,9},{2,6},{6,2},{1... | collective-permute-start | bytes 1179656 | tf_op jit(solution)/shard_map/ppermute | solution.py:190
  46.0 7.9 %dense_low.1 = (bf16[512,2048]{1,0:T(8,128)(2,1)}, bf16[512,2048]{1,0:T(8,128)(2,1)}, f32[8,128]{1,0:T(8,128)}) custom-call(f32[16,8,21]{2,1,0:T(8,128)} %fusion.4.lam, bf16[512,2048]{1,0:T(8,128)(2,1)} %g.1, bf16[512,2048]{1,0:T(8,128)(2,1)} %v.1, bf16[512,2048]{1,0:T(8,128)(2,1)} %k.1, bf16[512,2048]{1,0:T(8,128)(2,1)} %q.1, bf16[3,4,128,128]{3,2,1,0:T(8,128)(2,1)} %copy-done.1), custom_call_target="tpu_custom_call" | custom-call | flops 2147483648 | bytes 6291456 | tf_op jit(solution)/shard_map/dense_low/pallas_call | solution.py:168
  53.9 1.2 %slice.72 = f32[1,1]{1,0:T(1,128)} slice(f32[8,128]{1,0:T(8,128)} %get-tuple-element.17), slice={[0:1], [0:1]} | slice | bytes 8 | tf_op jit(solution)/shard_map/slice | solution.py:224
  55.1 1.6 %add_convert_fusion.4 = bf16[2,4,128,128]{3,2,1,0:T(8,128)(2,1)S(1)} fusion(bf16[3,4,128,128]{3,2,1,0:T(8,128)(2,1)S(1)} %collective-permute-done.2, bf16[3,4,128,128]{3,2,1,0:T(8,128)(2,1)} %copy-done.1, f32[]{:T(128)} %bitcast.4), kind=kLoop, calls=%fused_computation.9 | loop fusion | flops 655360 | bytes 786436 | tf_op jit(solution)/shard_map/convert_element_type | solution.py:249
  56.7 2.6 %collective-permute-start.3 = (bf16[4,128,128]{2,1,0:T(8,128)(2,1)S(1)}, bf16[4,128,128]{2,1,0:T(8,128)(2,1)S(1)}, u32[]{:S(2)}, u32[]{:S(2)}) collective-permute-start(bf16[4,128,128]{2,1,0:T(8,128)(2,1)S(1)} %fusion.3), channel_id=1, source_target_pairs={{0,8},{4,12},{8,0},{12,4},{1,9},{5,13},{9,1},{13,5},{2,10},{6,14},... | collective-permute-start | bytes 393224 | tf_op jit(solution)/shard_map/ppermute | solution.py:190
  59.4 1.3 %fusion = bf16[16,128,128]{2,1,0:T(8,128)(2,1)S(1)} fusion(bf16[5,16,128,128]{3,2,1,0:T(8,128)(2,1)} %states.1, pred[]{:T(512)S(6)} %eq.46), kind=kLoop, calls=%fused_computation.7 | loop fusion | flops 262144 | bytes 1572865 | tf_op jit(solution)/shard_map/jit(_where)/select_n | solution.py:197
  60.6 0.1 collective-permute-start.4
  60.7 4.4 %collective-permute-done.3 = bf16[4,128,128]{2,1,0:T(8,128)(2,1)S(1)} collective-permute-done((bf16[4,128,128]{2,1,0:T(8,128)(2,1)S(1)}, bf16[4,128,128]{2,1,0:T(8,128)(2,1)S(1)}, u32[]{:S(2)}, u32[]{:S(2)}) %collective-permute-start.3) | collective-permute-done | bytes 131104 | tf_op jit(solution)/shard_map/ppermute | solution.py:190
  65.2 0.1 fusion.2
  65.3 0.0 copy-start.4
  65.3 1.6 %collective-permute-start.5 = (bf16[3,4,128,128]{3,2,1,0:T(8,128)(2,1)S(1)}, bf16[3,4,128,128]{3,2,1,0:T(8,128)(2,1)}, u32[]{:S(2)}, u32[]{:S(2)}) collective-permute-start(bf16[3,4,128,128]{3,2,1,0:T(8,128)(2,1)S(1)} %pad_maximum_fusion.2.refs_2_), channel_id=1, source_target_pairs={{0,2},{1,3},{2,0},{3,1},{4,6},{5,7},{6,4},{7,5},{8,10},{9,11},{10,... | collective-permute-start | bytes 1179656 | tf_op jit(solution)/shard_map/ppermute | solution.py:188
  66.8 1.0 slice.96
  67.8 0.0 collective-permute-done.4.refs_3_.x0
  67.8 0.8 copy-done.2
  68.6 7.9 %dense_high.1 = (bf16[512,2048]{1,0:T(8,128)(2,1)}, bf16[512,2048]{1,0:T(8,128)(2,1)}, f32[8,128]{1,0:T(8,128)}) custom-call(f32[16,8,21]{2,1,0:T(8,128)} %fusion.4.lam, bf16[512,2048]{1,0:T(8,128)(2,1)} %g.1, bf16[512,2048]{1,0:T(8,128)(2,1)} %v.1, bf16[512,2048]{1,0:T(8,128)(2,1)} %k.1, ...), custom_call_target="tpu_custom_call", output_to_operand_aliasing={{0}: (5, {}), {1}: (6, {})} | custom-call | flops 2147483648 | bytes 6291456 | tf_op jit(solution)/shard_map/dense_high/pallas_call | solution.py:168
  76.6 1.2 %slice.79 = f32[1,1]{1,0:T(1,128)} slice(f32[8,128]{1,0:T(8,128)} %get-tuple-element.21), slice={[0:1], [0:1]} | slice | bytes 8 | tf_op jit(solution)/shard_map/slice | solution.py:224
  77.8 1.7 %add_convert_fusion.1 = bf16[3,4,128,128]{3,2,1,0:T(8,128)(2,1)S(1)} fusion(bf16[3,4,128,128]{3,2,1,0:T(8,128)(2,1)} %collective-permute-done.5, f32[]{:T(128)} %bitcast.11), kind=kLoop, calls=%fused_computation.3 | loop fusion | flops 589824 | bytes 786436 | tf_op jit(solution)/shard_map/convert_element_type | solution.py:251
  79.5 0.1 maximum_select_fusion
  79.6 0.0 copy-start.3
  79.7 0.1 add_convert_fusion.3
  79.8 0.1 pad_maximum_fusion.ours
  79.9 0.1 collective-permute-start.6
  80.0 0.7 pad_add_fusion.pick
  80.8 0.7 slice_multiply_fusion.lam
  81.5 1.2 %collective-permute-done.6.theirs = bf16[4,8,128,128]{3,2,1,0:T(8,128)(2,1)S(1)} collective-permute-done((bf16[4,8,128,128]{3,2,1,0:T(8,128)(2,1)S(1)}, bf16[4,8,128,128]{3,2,1,0:T(8,128)(2,1)S(1)}, u32[]{:S(2)}, u32[]{:S(2)}) %collective-permute-start.6) | collective-permute-done | bytes 1048608 | tf_op jit(solution)/shard_map/ppermute | solution.py:188
  82.6 1.0 %copy-done.5 = bf16[4,8,128,128]{3,2,1,0:T(8,128)(2,1)} copy-done((bf16[4,8,128,128]{3,2,1,0:T(8,128)(2,1)}, bf16[4,8,128,128]{3,2,1,0:T(8,128)(2,1)S(1)}, u32[]{:S(2)}) %copy-start.5) | copy-done | bytes 1048600
  83.6 14.2 %cross.1 = (bf16[512,2048]{1,0:T(8,128)(2,1)}, bf16[512,2048]{1,0:T(8,128)(2,1)}, bf16[512,2048]{1,0:T(8,128)(2,1)}, bf16[512,2048]{1,0:T(8,128)(2,1)}) custom-call(f32[16,8,4]{2,1,0:T(8,128)} %slice_multiply_fusion.lam, s32[9]{0:T(128)} %pad_add_fusion.pick, bf16[512,2048]{1,0:T(8,128)(2,1)} %q.1, bf16[512,2048]{1,0:T(8,128)(2,1)} %k.1, ...), custom_call_target="tpu_custom_call" | custom-call | tf_op jit(solution)/shard_map/cross/pallas_call | solution.py:267
  (20 shorter events, 0.2 us)
Async XLA Ops:
  20.2 2.9 %collective-permute-start = (bf16[4,8,128,128]{3,2,1,0:T(8,128)(2,1)S(1)}, bf16[4,8,128,128]{3,2,1,0:T(8,128)(2,1)}, u32[]{:S(2)}, u32[]{:S(2)}) collective-permute-start(bf16[4,8,128,128]{3,2,1,0:T(8,128)(2,1)S(1)} %constant_dynamic-slice_fusion.1), channel_id=1, source_target_pairs={{0,1},{1,0},{2,3},{3,2},{4,5},{5,4},{6,7},{7,6},{8,9},{9,8},{10,11... | collective-permute-start | bytes 3145736 | tf_op jit(solution)/shard_map/ppermute | solution.py:188
  24.9 2.1 %copy-start.6 = (bf16[5,4,128,128]{3,2,1,0:T(8,128)(2,1)}, bf16[5,4,128,128]{3,2,1,0:T(8,128)(2,1)S(1)}, u32[]{:S(2)}) copy-start(bf16[5,4,128,128]{3,2,1,0:T(8,128)(2,1)S(1)} %pad_maximum_fusion.1.refs_0_) | copy-start | bytes 1966084
  24.9 17.4 %collective-permute-start.1 = (bf16[5,4,128,128]{3,2,1,0:T(8,128)(2,1)S(1)}, bf16[5,4,128,128]{3,2,1,0:T(8,128)(2,1)}, u32[]{:S(2)}, u32[]{:S(2)}) collective-permute-start(bf16[5,4,128,128]{3,2,1,0:T(8,128)(2,1)S(1)} %pad_maximum_fusion.1.refs_0_), channel_id=1, source_target_pairs={{0,2},{1,3},{2,0},{3,1},{4,6},{5,7},{6,4},{7,5},{8,10},{9,11},{10,... | collective-permute-start | bytes 1966088 | tf_op jit(solution)/shard_map/ppermute | solution.py:188
  44.1 1.9 %copy-start.1 = (bf16[3,4,128,128]{3,2,1,0:T(8,128)(2,1)}, bf16[3,4,128,128]{3,2,1,0:T(8,128)(2,1)S(1)}, u32[]{:S(2)}) copy-start(bf16[3,4,128,128]{3,2,1,0:T(8,128)(2,1)S(1)} %add_convert_fusion.2.refs_0_) | copy-start | bytes 1179652
  44.1 11.0 %collective-permute-start.2 = (bf16[3,4,128,128]{3,2,1,0:T(8,128)(2,1)S(1)}, bf16[3,4,128,128]{3,2,1,0:T(8,128)(2,1)S(1)}, u32[]{:S(2)}, u32[]{:S(2)}) collective-permute-start(bf16[3,4,128,128]{3,2,1,0:T(8,128)(2,1)S(1)} %add_convert_fusion.2.refs_0_), channel_id=1, source_target_pairs={{0,4},{4,0},{8,12},{12,8},{1,5},{5,1},{9,13},{13,9},{2,6},{6,2},{1... | collective-permute-start | bytes 1179656 | tf_op jit(solution)/shard_map/ppermute | solution.py:190
  56.7 8.4 %collective-permute-start.3 = (bf16[4,128,128]{2,1,0:T(8,128)(2,1)S(1)}, bf16[4,128,128]{2,1,0:T(8,128)(2,1)S(1)}, u32[]{:S(2)}, u32[]{:S(2)}) collective-permute-start(bf16[4,128,128]{2,1,0:T(8,128)(2,1)S(1)} %fusion.3), channel_id=1, source_target_pairs={{0,8},{4,12},{8,0},{12,4},{1,9},{5,13},{9,1},{13,5},{2,10},{6,14},... | collective-permute-start | bytes 393224 | tf_op jit(solution)/shard_map/ppermute | solution.py:190
  60.6 7.2 %collective-permute-start.4 = (bf16[16,128,128]{2,1,0:T(8,128)(2,1)S(1)}, bf16[16,128,128]{2,1,0:T(8,128)(2,1)S(1)}, u32[]{:S(2)}, u32[]{:S(2)}) collective-permute-start(bf16[16,128,128]{2,1,0:T(8,128)(2,1)S(1)} %fusion), channel_id=1, source_target_pairs={{0,1},{1,0},{2,3},{3,2},{4,5},{5,4},{6,7},{7,6},{8,9},{9,8},{10,11... | collective-permute-start | bytes 1572872 | tf_op jit(solution)/shard_map/ppermute | solution.py:188
  65.3 2.6 %copy-start.4 = (bf16[3,4,128,128]{3,2,1,0:T(8,128)(2,1)}, bf16[3,4,128,128]{3,2,1,0:T(8,128)(2,1)S(1)}, u32[]{:S(2)}) copy-start(bf16[3,4,128,128]{3,2,1,0:T(8,128)(2,1)S(1)} %pad_maximum_fusion.2.refs_2_) | copy-start | bytes 1179652
  65.3 12.5 %collective-permute-start.5 = (bf16[3,4,128,128]{3,2,1,0:T(8,128)(2,1)S(1)}, bf16[3,4,128,128]{3,2,1,0:T(8,128)(2,1)}, u32[]{:S(2)}, u32[]{:S(2)}) collective-permute-start(bf16[3,4,128,128]{3,2,1,0:T(8,128)(2,1)S(1)} %pad_maximum_fusion.2.refs_2_), channel_id=1, source_target_pairs={{0,2},{1,3},{2,0},{3,1},{4,6},{5,7},{6,4},{7,5},{8,10},{9,11},{10,... | collective-permute-start | bytes 1179656 | tf_op jit(solution)/shard_map/ppermute | solution.py:188
  67.8 0.8 copy-start.2
  79.6 1.1 %copy-start.3 = (f32[16,8,21]{2,1,0:T(8,128)S(1)}, f32[16,8,21]{2,1,0:T(8,128)}, u32[]{:S(2)}) copy-start(f32[16,8,21]{2,1,0:T(8,128)} %fusion.4.lam) | copy-start | bytes 32260
  79.9 3.7 %copy-start = (bf16[4,8,128,128]{3,2,1,0:T(8,128)(2,1)}, bf16[4,8,128,128]{3,2,1,0:T(8,128)(2,1)S(1)}, u32[]{:S(2)}) copy-start(bf16[4,8,128,128]{3,2,1,0:T(8,128)(2,1)S(1)} %pad_maximum_fusion.ours) | copy-start | bytes 3145732
  79.9 2.7 %collective-permute-start.6 = (bf16[4,8,128,128]{3,2,1,0:T(8,128)(2,1)S(1)}, bf16[4,8,128,128]{3,2,1,0:T(8,128)(2,1)S(1)}, u32[]{:S(2)}, u32[]{:S(2)}) collective-permute-start(bf16[4,8,128,128]{3,2,1,0:T(8,128)(2,1)S(1)} %pad_maximum_fusion.ours), channel_id=1, source_target_pairs={{0,1},{1,0},{2,3},{3,2},{4,5},{5,4},{6,7},{7,6},{8,9},{9,8},{10,11... | collective-permute-start | bytes 3145736 | tf_op jit(solution)/shard_map/ppermute | solution.py:188
  82.6 1.0 %copy-start.5 = (bf16[4,8,128,128]{3,2,1,0:T(8,128)(2,1)}, bf16[4,8,128,128]{3,2,1,0:T(8,128)(2,1)S(1)}, u32[]{:S(2)}) copy-start(bf16[4,8,128,128]{3,2,1,0:T(8,128)(2,1)S(1)} %collective-permute-done.6.theirs) | copy-start | bytes 3145732

commit v5 on v4

--- a/solution.py
+++ b/solution.py
@@ -17,6 +17,7 @@
 NN = (((1,), (0,)), ((), ()))
 VMEM_LIMIT = 62 * 1024 * 1024
 GROUP = 2
+WIDE = 4
 
 
 def mm(a, b, dims):
@@ -94,11 +95,11 @@
     bits, lam, pick, q, k, v, g, o_in, dq_in, dk_in, dv_in, x0, ours, theirs, o, dq, dk, dv
 ):
     tok = q.shape[0]
-    width = q.shape[1] // GROUP
+    width = q.shape[1] // WIDE
     own = pick[pl.program_id(0)] == 1
     lower = pick[pl.num_programs(0)] == 1
-    for n in range(GROUP):
-        head = pl.program_id(0) * GROUP + n
+    for n in range(WIDE):
+        head = pl.program_id(0) * WIDE + n
         lanes = slice(n * width, (n + 1) * width)
         rest = [jnp.where(own, ours[j, n], theirs[j, n]) for j in range(bits)]
         back = rest[bits - 1].astype(F32) + jnp.where(lower, x0[n].astype(F32), 0.0)
@@ -258,17 +259,18 @@
     theirs = swap(ours, 0)
     o_part, dv_part = dense_parts["out"]
     dq_part, dk_part = dense_parts["grad"]
-    steps = half // GROUP
-    pick = (jnp.arange(groups, dtype=jnp.int32) // steps == core).astype(jnp.int32)
+    steps = half // WIDE
+    pick = (jnp.arange(heads // WIDE, dtype=jnp.int32) // steps == core).astype(jnp.int32)
     pick = jnp.concatenate([pick, (1 - core).astype(jnp.int32)[None]])
 
-    mat_spec = pl.BlockSpec((GROUP, width, width), lambda h: (h, 0, 0))
-    half_spec = pl.BlockSpec((bits, GROUP, width, width), lambda h: (0, h % steps, 0, 0))
+    wide_spec = pl.BlockSpec((tok, WIDE * width), lambda h: (0, h))
+    mat_spec = pl.BlockSpec((WIDE, width, width), lambda h: (h, 0, 0))
+    half_spec = pl.BlockSpec((bits, WIDE, width, width), lambda h: (0, h % steps, 0, 0))
     return pl.pallas_call(
         functools.partial(cross_kernel, bits),
-        grid=(heads // GROUP,),
-        in_specs=[smem] * 2 + [row_spec] * 8 + [mat_spec, half_spec, half_spec],
-        out_specs=[row_spec] * 4,
+        grid=(heads // WIDE,),
+        in_specs=[smem] * 2 + [wide_spec] * 8 + [mat_spec, half_spec, half_spec],
+        out_specs=[wide_spec] * 4,
         out_shape=[row_shape] * 4,
         compiler_params=params,
         name="cross",

time: 99 us -> 97.2 us (0.982)
  Pallas kernels: 52.5 us -> 50.8 us
    pallas_call x1, Pallas kernels: 14.2 us -> 12.5 us  [shards(): pl.pallas_call(functools.partial(cross_kernel, bits), grid=(heads // WIDE...]
where the time goes in v5:
time: 97.2 us; the launch traced here: 96.2 us
  Pallas kernels  50.8 us (52%)
  other arithmetic  10.8 us (11%)
  local copies, waits for them, and re-layouts  9.79 us (10%)
  waiting for transfers between devices  8.98 us (9%)
  starting transfers between devices  8.72 us (9%)
  blocking collectives  6.15 us (6%)
    pallas_call x3, Pallas kernels, dense(): pl.pallas_call(functools.partial(dense_kernel, first), grid=(count,), in_...  29.1 us
    pallas_call x1, Pallas kernels, shards(): pl.pallas_call(functools.partial(cross_kernel, bits), grid=(heads // WIDE...  12.5 us
    pallas_call x1, Pallas kernels, shards(): pl.pallas_call(functools.partial(state_kernel, bits, low), grid=(heads //...  9.21 us
    all_gather x1, blocking collectives, shards(): table = lax.all_gather(level_table, 'head', axis=2, tiled=True)  6.15 us
    ppermute x5, waiting for transfers between devices, swap(): return lax.ppermute(array, 'head', pairs)  4.55 us
    ppermute x2, starting transfers between devices, swap(): return lax.ppermute(array, 'ctx', [(i, i ^ step) for i in range(ctx_n)])  4.54 us
    ppermute x2, waiting for transfers between devices, swap(): return lax.ppermute(array, 'ctx', [(i, i ^ step) for i in range(ctx_n)])  4.43 us
    ppermute x5, starting transfers between devices, swap(): return lax.ppermute(array, 'head', pairs)  4.18 us
  transfers between devices with their start and end apart: 7, of which 4 were waited for; matrix products, arithmetic and copies ran while one was open for 8% of the time, Pallas kernels for 30%

profile of v5, /device:TPU:0, one launch (start us, length us, event | category | flops | bytes accessed | tf_op | source)
XLA Modules:
  0.0 96.2 jit_solution(10358162838727131570)
XLA Ops:
  0.7 0.7 dynamic_slice.15
  1.4 0.1 fusion.5
  1.5 0.7 copy.15
  2.2 6.1 %all_gather.3 = f32[8,21,16]{1,0,2:T(8,128)S(1)} all-gather(f32[8,21,4]{1,0,2:T(8,128)S(1)} %copy.15), channel_id=1, replica_groups=mesh['grp'=2,'ctx'=4,'head'=4] {'head'}, dimensions={2}, use_global_device_ids=true | all-gather | bytes 13440 | tf_op jit(solution)/shard_map/all_gather | solution.py:136
  8.3 0.1 multiply_reduce_fusion
  8.5 0.7 fusion.4.lam
  9.1 9.2 %states.1 = bf16[5,16,128,128]{3,2,1,0:T(8,128)(2,1)} custom-call(f32[16,8,21]{2,1,0:T(8,128)} %fusion.4.lam, bf16[512,2048]{1,0:T(8,128)(2,1)} %q.1, bf16[512,2048]{1,0:T(8,128)(2,1)} %k.1, bf16[512,2048]{1,0:T(8,128)(2,1)} %v.1, bf16[512,2048]{1,0:T(8,128)(2,1)} %g.1), custom_call_target="tpu_custom_call" | custom-call | tf_op jit(solution)/shard_map/states/pallas_call | solution.py:154
  18.3 1.7 %slice.83 = bf16[4,16,128,128]{3,2,1,0:T(8,128)(2,1)S(1)} slice(bf16[5,16,128,128]{3,2,1,0:T(8,128)(2,1)} %states.1), slice={[0:4], [0:16], [0:128], [0:128]} | slice | bytes 4194304 | tf_op jit(solution)/shard_map/slice | solution.py:202
  20.1 0.1 constant_dynamic-slice_fusion.1
  20.2 0.4 collective-permute-start
  20.6 2.5 %collective-permute-done = bf16[4,8,128,128]{3,2,1,0:T(8,128)(2,1)} collective-permute-done((bf16[4,8,128,128]{3,2,1,0:T(8,128)(2,1)S(1)}, bf16[4,8,128,128]{3,2,1,0:T(8,128)(2,1)}, u32[]{:S(2)}, u32[]{:S(2)}) %collective-permute-start) | collective-permute-done | bytes 1048608 | tf_op jit(solution)/shard_map/ppermute | solution.py:189
  23.1 1.6 %add_convert_fusion = bf16[4,8,128,128]{3,2,1,0:T(8,128)(2,1)S(1)} fusion(bf16[4,8,128,128]{3,2,1,0:T(8,128)(2,1)} %collective-permute-done, bf16[4,16,128,128]{3,2,1,0:T(8,128)(2,1)S(1)} %slice.83, s32[]{:T(128)S(6)} %select_n.95), kind=kLoop, calls=%fused_computation | loop fusion | flops 2097152 | bytes 3145732 | tf_op jit(solution)/shard_map/convert_element_type | solution.py:203
  24.6 0.1 slice.86
  24.8 0.1 pad_maximum_fusion.1.refs_0_
  24.9 0.0 copy-start.6
  24.9 2.1 %collective-permute-start.1 = (bf16[5,4,128,128]{3,2,1,0:T(8,128)(2,1)S(1)}, bf16[5,4,128,128]{3,2,1,0:T(8,128)(2,1)}, u32[]{:S(2)}, u32[]{:S(2)}) collective-permute-start(bf16[5,4,128,128]{3,2,1,0:T(8,128)(2,1)S(1)} %pad_maximum_fusion.1.refs_0_), channel_id=1, source_target_pairs={{0,2},{1,3},{2,0},{3,1},{4,6},{5,7},{6,4},{7,5},{8,10},{9,11},{10,... | collective-permute-start | bytes 1966088 | tf_op jit(solution)/shard_map/ppermute | solution.py:189
  27.0 13.2 %dense_out.1 = (bf16[512,2048]{1,0:T(8,128)(2,1)}, bf16[512,2048]{1,0:T(8,128)(2,1)}, f32[8,128]{1,0:T(8,128)}) custom-call(f32[16,8,21]{2,1,0:T(8,128)} %fusion.4.lam, bf16[512,2048]{1,0:T(8,128)(2,1)} %q.1, bf16[512,2048]{1,0:T(8,128)(2,1)} %k.1, bf16[512,2048]{1,0:T(8,128)(2,1)} %v.1, bf16[512,2048]{1,0:T(8,128)(2,1)} %g.1, bf16[5,4,128,128]{3,2,1,0:T(8,128)(2,1)} %copy-done.6), custom_call_target="tpu_custom_call" | custom-call | flops 4294967296 | bytes 12582912 | tf_op jit(solution)/shard_map/dense_out/pallas_call | solution.py:169
  40.2 1.2 %slice.68 = f32[1,1]{1,0:T(1,128)} slice(f32[8,128]{1,0:T(8,128)} %get-tuple-element.14), slice={[0:1], [0:1]} | slice | bytes 8 | tf_op jit(solution)/shard_map/slice | solution.py:225
  41.4 0.9 collective-permute-done.1
  42.3 1.8 %add_convert_fusion.2.refs_0_ = bf16[3,4,128,128]{3,2,1,0:T(8,128)(2,1)S(1)} fusion(bf16[5,4,128,128]{3,2,1,0:T(8,128)(2,1)} %collective-permute-done.1, f32[]{:T(128)} %bitcast.3, bf16[3,8,128,128]{3,2,1,0:T(8,128)(2,1)S(1)} %slice.86, s32[]{:T(128)S(6)} %select_n.100), kind=kLoop, calls=%fused_computation.4 | loop fusion | flops 983040 | bytes 1179656 | tf_op jit(solution)/shard_map/convert_element_type | solution.py:236
  44.1 0.0 copy-start.1
  44.1 1.9 %collective-permute-start.2 = (bf16[3,4,128,128]{3,2,1,0:T(8,128)(2,1)S(1)}, bf16[3,4,128,128]{3,2,1,0:T(8,128)(2,1)S(1)}, u32[]{:S(2)}, u32[]{:S(2)}) collective-permute-start(bf16[3,4,128,128]{3,2,1,0:T(8,128)(2,1)S(1)} %add_convert_fusion.2.refs_0_), channel_id=1, source_target_pairs={{0,4},{4,0},{8,12},{12,8},{1,5},{5,1},{9,13},{13,9},{2,6},{6,2},{1... | collective-permute-start | bytes 1179656 | tf_op jit(solution)/shard_map/ppermute | solution.py:191
  46.0 7.9 %dense_low.1 = (bf16[512,2048]{1,0:T(8,128)(2,1)}, bf16[512,2048]{1,0:T(8,128)(2,1)}, f32[8,128]{1,0:T(8,128)}) custom-call(f32[16,8,21]{2,1,0:T(8,128)} %fusion.4.lam, bf16[512,2048]{1,0:T(8,128)(2,1)} %g.1, bf16[512,2048]{1,0:T(8,128)(2,1)} %v.1, bf16[512,2048]{1,0:T(8,128)(2,1)} %k.1, bf16[512,2048]{1,0:T(8,128)(2,1)} %q.1, bf16[3,4,128,128]{3,2,1,0:T(8,128)(2,1)} %copy-done.1), custom_call_target="tpu_custom_call" | custom-call | flops 2147483648 | bytes 6291456 | tf_op jit(solution)/shard_map/dense_low/pallas_call | solution.py:169
  53.9 1.2 %slice.72 = f32[1,1]{1,0:T(1,128)} slice(f32[8,128]{1,0:T(8,128)} %get-tuple-element.17), slice={[0:1], [0:1]} | slice | bytes 8 | tf_op jit(solution)/shard_map/slice | solution.py:225
  55.1 1.6 %add_convert_fusion.4 = bf16[2,4,128,128]{3,2,1,0:T(8,128)(2,1)S(1)} fusion(bf16[3,4,128,128]{3,2,1,0:T(8,128)(2,1)S(1)} %collective-permute-done.2, bf16[3,4,128,128]{3,2,1,0:T(8,128)(2,1)} %copy-done.1, f32[]{:T(128)} %bitcast.4), kind=kLoop, calls=%fused_computation.9 | loop fusion | flops 655360 | bytes 786436 | tf_op jit(solution)/shard_map/convert_element_type | solution.py:250
  56.7 2.6 %collective-permute-start.3 = (bf16[4,128,128]{2,1,0:T(8,128)(2,1)S(1)}, bf16[4,128,128]{2,1,0:T(8,128)(2,1)S(1)}, u32[]{:S(2)}, u32[]{:S(2)}) collective-permute-start(bf16[4,128,128]{2,1,0:T(8,128)(2,1)S(1)} %fusion.3), channel_id=1, source_target_pairs={{0,8},{4,12},{8,0},{12,4},{1,9},{5,13},{9,1},{13,5},{2,10},{6,14},... | collective-permute-start | bytes 393224 | tf_op jit(solution)/shard_map/ppermute | solution.py:191
  59.4 1.3 %fusion = bf16[16,128,128]{2,1,0:T(8,128)(2,1)S(1)} fusion(bf16[5,16,128,128]{3,2,1,0:T(8,128)(2,1)} %states.1, pred[]{:T(512)S(6)} %eq.46), kind=kLoop, calls=%fused_computation.7 | loop fusion | flops 262144 | bytes 1572865 | tf_op jit(solution)/shard_map/jit(_where)/select_n | solution.py:198
  60.6 0.1 collective-permute-start.4
  60.7 4.4 %collective-permute-done.3 = bf16[4,128,128]{2,1,0:T(8,128)(2,1)S(1)} collective-permute-done((bf16[4,128,128]{2,1,0:T(8,128)(2,1)S(1)}, bf16[4,128,128]{2,1,0:T(8,128)(2,1)S(1)}, u32[]{:S(2)}, u32[]{:S(2)}) %collective-permute-start.3) | collective-permute-done | bytes 131104 | tf_op jit(solution)/shard_map/ppermute | solution.py:191
  65.2 0.1 fusion.2
  65.3 0.0 copy-start.4
  65.3 1.6 %collective-permute-start.5 = (bf16[3,4,128,128]{3,2,1,0:T(8,128)(2,1)S(1)}, bf16[3,4,128,128]{3,2,1,0:T(8,128)(2,1)}, u32[]{:S(2)}, u32[]{:S(2)}) collective-permute-start(bf16[3,4,128,128]{3,2,1,0:T(8,128)(2,1)S(1)} %pad_maximum_fusion.2.refs_2_), channel_id=1, source_target_pairs={{0,2},{1,3},{2,0},{3,1},{4,6},{5,7},{6,4},{7,5},{8,10},{9,11},{10,... | collective-permute-start | bytes 1179656 | tf_op jit(solution)/shard_map/ppermute | solution.py:189
  66.8 1.0 %slice.96 = bf16[2,4,128,128]{3,2,1,0:T(8,128)(2,1)S(1)} slice(bf16[5,4,128,128]{3,2,1,0:T(8,128)(2,1)} %collective-permute-done.1), slice={[0:2], [0:4], [0:128], [0:128]} | slice | bytes 524288 | tf_op jit(solution)/shard_map/slice | solution.py:235
  67.8 0.0 collective-permute-done.4.refs_3_.x0
  67.8 0.8 copy-done.2
  68.6 7.9 %dense_high.1 = (bf16[512,2048]{1,0:T(8,128)(2,1)}, bf16[512,2048]{1,0:T(8,128)(2,1)}, f32[8,128]{1,0:T(8,128)}) custom-call(f32[16,8,21]{2,1,0:T(8,128)} %fusion.4.lam, bf16[512,2048]{1,0:T(8,128)(2,1)} %g.1, bf16[512,2048]{1,0:T(8,128)(2,1)} %v.1, bf16[512,2048]{1,0:T(8,128)(2,1)} %k.1, ...), custom_call_target="tpu_custom_call", output_to_operand_aliasing={{0}: (5, {}), {1}: (6, {})} | custom-call | flops 2147483648 | bytes 6291456 | tf_op jit(solution)/shard_map/dense_high/pallas_call | solution.py:169
  76.6 1.2 %slice.79 = f32[1,1]{1,0:T(1,128)} slice(f32[8,128]{1,0:T(8,128)} %get-tuple-element.21), slice={[0:1], [0:1]} | slice | bytes 8 | tf_op jit(solution)/shard_map/slice | solution.py:225
  77.8 1.7 %add_convert_fusion.1 = bf16[3,4,128,128]{3,2,1,0:T(8,128)(2,1)S(1)} fusion(bf16[3,4,128,128]{3,2,1,0:T(8,128)(2,1)} %collective-permute-done.5, f32[]{:T(128)} %bitcast.11), kind=kLoop, calls=%fused_computation.3 | loop fusion | flops 589824 | bytes 786436 | tf_op jit(solution)/shard_map/convert_element_type | solution.py:252
  79.5 0.1 maximum_select_fusion
  79.6 0.0 copy-start.3
  79.7 0.1 add_convert_fusion.3
  79.8 0.1 pad_maximum_fusion.ours
  79.9 0.1 collective-permute-start.6
  80.0 0.7 pad_add_fusion.pick
  80.8 0.7 slice_multiply_fusion.lam
  81.5 1.2 %collective-permute-done.6.theirs = bf16[4,8,128,128]{3,2,1,0:T(8,128)(2,1)S(1)} collective-permute-done((bf16[4,8,128,128]{3,2,1,0:T(8,128)(2,1)S(1)}, bf16[4,8,128,128]{3,2,1,0:T(8,128)(2,1)S(1)}, u32[]{:S(2)}, u32[]{:S(2)}) %collective-permute-start.6) | collective-permute-done | bytes 1048608 | tf_op jit(solution)/shard_map/ppermute | solution.py:189
  82.6 1.0 %copy-done.5 = bf16[4,8,128,128]{3,2,1,0:T(8,128)(2,1)} copy-done((bf16[4,8,128,128]{3,2,1,0:T(8,128)(2,1)}, bf16[4,8,128,128]{3,2,1,0:T(8,128)(2,1)S(1)}, u32[]{:S(2)}) %copy-start.5) | copy-done | bytes 1048600
  83.6 12.5 %cross.1 = (bf16[512,2048]{1,0:T(8,128)(2,1)}, bf16[512,2048]{1,0:T(8,128)(2,1)}, bf16[512,2048]{1,0:T(8,128)(2,1)}, bf16[512,2048]{1,0:T(8,128)(2,1)}) custom-call(f32[16,8,4]{2,1,0:T(8,128)} %slice_multiply_fusion.lam, s32[5]{0:T(128)} %pad_add_fusion.pick, bf16[512,2048]{1,0:T(8,128)(2,1)} %q.1, bf16[512,2048]{1,0:T(8,128)(2,1)} %k.1, ...), custom_call_target="tpu_custom_call" | custom-call | tf_op jit(solution)/shard_map/cross/pallas_call | solution.py:269
  (20 shorter events, 0.2 us)
Async XLA Ops:
  20.2 2.9 %collective-permute-start = (bf16[4,8,128,128]{3,2,1,0:T(8,128)(2,1)S(1)}, bf16[4,8,128,128]{3,2,1,0:T(8,128)(2,1)}, u32[]{:S(2)}, u32[]{:S(2)}) collective-permute-start(bf16[4,8,128,128]{3,2,1,0:T(8,128)(2,1)S(1)} %constant_dynamic-slice_fusion.1), channel_id=1, source_target_pairs={{0,1},{1,0},{2,3},{3,2},{4,5},{5,4},{6,7},{7,6},{8,9},{9,8},{10,11... | collective-permute-start | bytes 3145736 | tf_op jit(solution)/shard_map/ppermute | solution.py:189
  24.9 2.1 %copy-start.6 = (bf16[5,4,128,128]{3,2,1,0:T(8,128)(2,1)}, bf16[5,4,128,128]{3,2,1,0:T(8,128)(2,1)S(1)}, u32[]{:S(2)}) copy-start(bf16[5,4,128,128]{3,2,1,0:T(8,128)(2,1)S(1)} %pad_maximum_fusion.1.refs_0_) | copy-start | bytes 1966084
  24.9 17.4 %collective-permute-start.1 = (bf16[5,4,128,128]{3,2,1,0:T(8,128)(2,1)S(1)}, bf16[5,4,128,128]{3,2,1,0:T(8,128)(2,1)}, u32[]{:S(2)}, u32[]{:S(2)}) collective-permute-start(bf16[5,4,128,128]{3,2,1,0:T(8,128)(2,1)S(1)} %pad_maximum_fusion.1.refs_0_), channel_id=1, source_target_pairs={{0,2},{1,3},{2,0},{3,1},{4,6},{5,7},{6,4},{7,5},{8,10},{9,11},{10,... | collective-permute-start | bytes 1966088 | tf_op jit(solution)/shard_map/ppermute | solution.py:189
  44.1 1.9 %copy-start.1 = (bf16[3,4,128,128]{3,2,1,0:T(8,128)(2,1)}, bf16[3,4,128,128]{3,2,1,0:T(8,128)(2,1)S(1)}, u32[]{:S(2)}) copy-start(bf16[3,4,128,128]{3,2,1,0:T(8,128)(2,1)S(1)} %add_convert_fusion.2.refs_0_) | copy-start | bytes 1179652
  44.1 11.0 %collective-permute-start.2 = (bf16[3,4,128,128]{3,2,1,0:T(8,128)(2,1)S(1)}, bf16[3,4,128,128]{3,2,1,0:T(8,128)(2,1)S(1)}, u32[]{:S(2)}, u32[]{:S(2)}) collective-permute-start(bf16[3,4,128,128]{3,2,1,0:T(8,128)(2,1)S(1)} %add_convert_fusion.2.refs_0_), channel_id=1, source_target_pairs={{0,4},{4,0},{8,12},{12,8},{1,5},{5,1},{9,13},{13,9},{2,6},{6,2},{1... | collective-permute-start | bytes 1179656 | tf_op jit(solution)/shard_map/ppermute | solution.py:191
  56.7 8.4 %collective-permute-start.3 = (bf16[4,128,128]{2,1,0:T(8,128)(2,1)S(1)}, bf16[4,128,128]{2,1,0:T(8,128)(2,1)S(1)}, u32[]{:S(2)}, u32[]{:S(2)}) collective-permute-start(bf16[4,128,128]{2,1,0:T(8,128)(2,1)S(1)} %fusion.3), channel_id=1, source_target_pairs={{0,8},{4,12},{8,0},{12,4},{1,9},{5,13},{9,1},{13,5},{2,10},{6,14},... | collective-permute-start | bytes 393224 | tf_op jit(solution)/shard_map/ppermute | solution.py:191
  60.6 7.2 %collective-permute-start.4 = (bf16[16,128,128]{2,1,0:T(8,128)(2,1)S(1)}, bf16[16,128,128]{2,1,0:T(8,128)(2,1)S(1)}, u32[]{:S(2)}, u32[]{:S(2)}) collective-permute-start(bf16[16,128,128]{2,1,0:T(8,128)(2,1)S(1)} %fusion), channel_id=1, source_target_pairs={{0,1},{1,0},{2,3},{3,2},{4,5},{5,4},{6,7},{7,6},{8,9},{9,8},{10,11... | collective-permute-start | bytes 1572872 | tf_op jit(solution)/shard_map/ppermute | solution.py:189
  65.3 2.6 %copy-start.4 = (bf16[3,4,128,128]{3,2,1,0:T(8,128)(2,1)}, bf16[3,4,128,128]{3,2,1,0:T(8,128)(2,1)S(1)}, u32[]{:S(2)}) copy-start(bf16[3,4,128,128]{3,2,1,0:T(8,128)(2,1)S(1)} %pad_maximum_fusion.2.refs_2_) | copy-start | bytes 1179652
  65.3 12.5 %collective-permute-start.5 = (bf16[3,4,128,128]{3,2,1,0:T(8,128)(2,1)S(1)}, bf16[3,4,128,128]{3,2,1,0:T(8,128)(2,1)}, u32[]{:S(2)}, u32[]{:S(2)}) collective-permute-start(bf16[3,4,128,128]{3,2,1,0:T(8,128)(2,1)S(1)} %pad_maximum_fusion.2.refs_2_), channel_id=1, source_target_pairs={{0,2},{1,3},{2,0},{3,1},{4,6},{5,7},{6,4},{7,5},{8,10},{9,11},{10,... | collective-permute-start | bytes 1179656 | tf_op jit(solution)/shard_map/ppermute | solution.py:189
  67.8 0.8 copy-start.2
  79.6 1.1 %copy-start.3 = (f32[16,8,21]{2,1,0:T(8,128)S(1)}, f32[16,8,21]{2,1,0:T(8,128)}, u32[]{:S(2)}) copy-start(f32[16,8,21]{2,1,0:T(8,128)} %fusion.4.lam) | copy-start | bytes 32260
  79.9 3.7 %copy-start = (bf16[4,8,128,128]{3,2,1,0:T(8,128)(2,1)}, bf16[4,8,128,128]{3,2,1,0:T(8,128)(2,1)S(1)}, u32[]{:S(2)}) copy-start(bf16[4,8,128,128]{3,2,1,0:T(8,128)(2,1)S(1)} %pad_maximum_fusion.ours) | copy-start | bytes 3145732
  79.9 2.7 %collective-permute-start.6 = (bf16[4,8,128,128]{3,2,1,0:T(8,128)(2,1)S(1)}, bf16[4,8,128,128]{3,2,1,0:T(8,128)(2,1)S(1)}, u32[]{:S(2)}, u32[]{:S(2)}) collective-permute-start(bf16[4,8,128,128]{3,2,1,0:T(8,128)(2,1)S(1)} %pad_maximum_fusion.ours), channel_id=1, source_target_pairs={{0,1},{1,0},{2,3},{3,2},{4,5},{5,4},{6,7},{7,6},{8,9},{9,8},{10,11... | collective-permute-start | bytes 3145736 | tf_op jit(solution)/shard_map/ppermute | solution.py:189
  82.6 1.0 %copy-start.5 = (bf16[4,8,128,128]{3,2,1,0:T(8,128)(2,1)}, bf16[4,8,128,128]{3,2,1,0:T(8,128)(2,1)S(1)}, u32[]{:S(2)}) copy-start(bf16[4,8,128,128]{3,2,1,0:T(8,128)(2,1)S(1)} %collective-permute-done.6.theirs) | copy-start | bytes 3145732
